TPU v7x, 256 devices: a whole 4x4x8 slice. The times are simulated.
256 devices in a mesh: seq: 8 (over x, core), tensor: 4 (over y), dp: 8 (over z).
Axes of the slice: x: 4, y: 4, z: 8, core: 2. Of those that a mesh axis runs over, the one named last changes fastest.
Arguments:
- inputs: bfloat16 [8, 2048, 3584], P('dp', 'seq'), may hold values from -6 to 6
- w_query: bfloat16 [3584, 2048], P(('seq', 'dp'), 'tensor'), may hold values from -0.09375 to 0.09375
- w_key: bfloat16 [3584, 1024], P(('seq', 'dp'), 'tensor'), may hold values from -0.09375 to 0.09375
- w_value: bfloat16 [3584, 1024], P(('seq', 'dp'), 'tensor'), may hold values from -0.09375 to 0.09375
- norm_gain: float32 [3584], replicated, may hold values from 0.1 to 1.9
- attn_grad: bfloat16 [8, 2048, 2048], P('dp', 'seq', 'tensor'), may hold values from -200 to 200
Outputs:
- grad_query: float32 [3584, 2048], P(('seq', 'dp'), 'tensor')
- grad_key: float32 [3584, 1024], P(('seq', 'dp'), 'tensor')
- grad_value: float32 [3584, 1024], P(('seq', 'dp'), 'tensor')
- input_grad: bfloat16 [8, 2048, 3584], P('dp', 'seq', 'tensor')
All inputs are finite; a program needn't handle non-finite values.
Results may differ from a plain program's by a relative error of at most 0.01.
Values may be sent and summed in bfloat16 or wider, within the bound.
No kernel may reach another device: no remote copies, remote signals or barrier semaphores. Data moves between devices by JAX's collectives and lax.ppermute only.
A program may use at most 64 MiB of HBM per device.

v0:
```python
import math

import jax
import jax.numpy as jnp
from jax import lax
from jax.sharding import PartitionSpec as P

D = 3584
H = 8
KVH = 4
HD = 256
WINDOW = 256


EPSILON = 1e-06
SOFTCAP = 50.0
CLIP_BOUND = 1.0
ROPE_BASE = 10000.0


def shifted(value, axis, steps):
    count = lax.axis_size(axis)
    leading, last = (max(0, -steps), min(count, count - steps))
    return lax.ppermute(value, axis, [(source, source + steps) for source in range(leading, last)])


def angles(positions, head_width):
    frequency = ROPE_BASE ** (-2.0 * jnp.arange(head_width // 2).astype(jnp.float32) / head_width)
    phases = positions.astype(jnp.float32)[:, None] * frequency[None, :]
    return (jnp.cos(phases)[:, None, :], jnp.sin(phases)[:, None, :])


def rotate(vectors, cosine, sine_part, direction):
    half_width = vectors.shape[-1] // 2
    first_half = vectors[..., :half_width]
    second_half = vectors[..., half_width:]
    return jnp.concatenate(
        [
            first_half * cosine - direction * second_half * sine_part,
            second_half * cosine + direction * first_half * sine_part,
        ],
        -1,
    )


def attend(queries, key_rows, value_rows, query_pos, key_pos, cotangent):
    query_count, head_count, head_width = queries.shape
    kv_heads = key_rows.shape[1]
    group_size = head_count // kv_heads
    grouped_query = queries.reshape(query_count, kv_heads, group_size, head_width)
    grouped_cot = cotangent.reshape(query_count, kv_heads, group_size, head_width)
    inv_scale = 1.0 / math.sqrt(head_width)
    logits = (
        jnp.einsum("tkgd,skd->kgts", grouped_query, key_rows, preferred_element_type=jnp.float32)
        * inv_scale
    )
    squash = jnp.tanh(logits / SOFTCAP)
    allowed = (
        (key_pos[None, :] <= query_pos[:, None])
        & (key_pos[None, :] > query_pos[:, None] - WINDOW)
        & (key_pos[None, :] >= 0)
    )
    exp_terms = jnp.where(allowed, jnp.exp(SOFTCAP * squash), 0.0)
    softmax = exp_terms / jnp.sum(exp_terms, -1, keepdims=True)
    probs_low = softmax.astype(jnp.bfloat16)
    dsoftmax = jnp.einsum(
        "tkgd,skd->kgts", grouped_cot, value_rows, preferred_element_type=jnp.float32
    )
    value_grads = jnp.einsum(
        "kgts,tkgd->skd", probs_low, grouped_cot, preferred_element_type=jnp.float32
    )
    row_delta = jnp.sum(softmax * dsoftmax, -1, keepdims=True)
    dlogits = (softmax * (dsoftmax - row_delta) * (1.0 - squash * squash) * inv_scale).astype(
        jnp.bfloat16
    )
    dquery = jnp.einsum("kgts,skd->tkgd", dlogits, key_rows, preferred_element_type=jnp.float32)
    key_grads = jnp.einsum(
        "kgts,tkgd->skd", dlogits, grouped_query, preferred_element_type=jnp.float32
    )
    return (dquery.reshape(query_count, head_count, head_width), key_grads, value_grads)


def local(inputs, w_query, w_key, w_value, norm_gain, attn_grad):
    widened = inputs[0].astype(jnp.float32)
    row_count = widened.shape[0]
    inverse_rms = lax.rsqrt(jnp.mean(widened * widened, -1) + EPSILON)
    normed = (widened * inverse_rms[:, None] * norm_gain[None, :]).astype(jnp.bfloat16)
    width_q = w_query.shape[1]
    width_k = w_key.shape[1]
    local_w = jnp.concatenate([w_query, w_key, w_value], 1)
    full_w = lax.all_gather(local_w, ("seq", "dp"), axis=0, tiled=True)
    projected = jnp.dot(normed, full_w, preferred_element_type=jnp.float32)
    start_row = lax.axis_index("seq") * row_count
    query_pos = start_row + jnp.arange(row_count, dtype=jnp.int32)
    key_pos = start_row - row_count + jnp.arange(2 * row_count, dtype=jnp.int32)
    cosine, sine_part = angles(query_pos, HD)
    heads_q = width_q // HD
    heads_k = width_k // HD
    rotated_query = rotate(
        projected[:, :width_q].reshape(row_count, heads_q, HD), cosine, sine_part, 1.0
    ).astype(jnp.bfloat16)
    rotated_keys = rotate(
        projected[:, width_q : width_q + width_k].reshape(row_count, heads_k, HD),
        cosine,
        sine_part,
        1.0,
    ).astype(jnp.bfloat16)
    value_rows = (
        projected[:, width_q + width_k :].reshape(row_count, heads_k, HD).astype(jnp.bfloat16)
    )
    keys_before, values_before = shifted((rotated_keys, value_rows), "seq", 1)
    dquery, key_ext_grad, value_ext_grad = attend(
        rotated_query,
        jnp.concatenate([keys_before, rotated_keys], 0),
        jnp.concatenate([values_before, value_rows], 0),
        query_pos,
        key_pos,
        attn_grad[0],
    )
    back_keys, back_values = shifted(
        (key_ext_grad[:row_count], value_ext_grad[:row_count]), "seq", -1
    )
    key_grads = key_ext_grad[row_count:] + back_keys
    value_grads = value_ext_grad[row_count:] + back_values
    dquery = rotate(dquery, cosine, sine_part, -1.0)
    key_grads = rotate(key_grads, cosine, sine_part, -1.0)
    d_out = jnp.concatenate(
        [
            dquery.reshape(row_count, width_q),
            key_grads.reshape(row_count, width_k),
            value_grads.reshape(row_count, width_k),
        ],
        1,
    ).astype(jnp.bfloat16)
    columns = lax.all_to_all(normed, "seq", split_axis=1, concat_axis=0, tiled=True)
    grad_rows = lax.dot_general(
        columns,
        lax.all_gather(d_out, "seq", axis=0, tiled=True),
        (((0,), (0,)), ((), ())),
        preferred_element_type=jnp.float32,
    )
    square_sum = lax.psum(jnp.sum(grad_rows * grad_rows), ("seq", "tensor"))
    grad_rms = jnp.sqrt(square_sum / (D * (H + 2 * KVH) * HD) + EPSILON)
    factor = CLIP_BOUND / jnp.maximum(grad_rms, CLIP_BOUND)
    clipped = lax.psum_scatter(factor * grad_rows, "dp", scatter_dimension=0, tiled=True)
    dnormed = lax.dot_general(
        d_out, full_w, (((1,), (1,)), ((), ())), preferred_element_type=jnp.float32
    )
    part_width = D // lax.axis_size("tensor")
    offset = lax.axis_index("tensor") * part_width
    summed_grad = lax.psum(dnormed, "tensor")
    scaled = norm_gain[None, :] * summed_grad
    mean_term = jnp.mean(widened * scaled, -1, keepdims=True)
    full_grad = (
        inverse_rms[:, None] * scaled
        - widened * (inverse_rms * inverse_rms * inverse_rms)[:, None] * mean_term
    )
    input_grad = lax.dynamic_slice_in_dim(full_grad, offset, part_width, 1)
    return (
        clipped[:, :width_q],
        clipped[:, width_q : width_q + width_k],
        clipped[:, width_q + width_k :],
        input_grad.astype(jnp.bfloat16)[None],
    )


def solution(mesh):
    return jax.shard_map(
        local,
        mesh=mesh,
        in_specs=(
            P("dp", "seq", None),
            P(("seq", "dp"), "tensor"),
            P(("seq", "dp"), "tensor"),
            P(("seq", "dp"), "tensor"),
            P(),
            P("dp", "seq", "tensor"),
        ),
        out_specs=(
            P(("seq", "dp"), "tensor"),
            P(("seq", "dp"), "tensor"),
            P(("seq", "dp"), "tensor"),
            P("dp", "seq", "tensor"),
        ),
        check_vma=False,
    )
```

profile of v0, /device:TPU:1, one launch (start us, length us, event | category | flops | bytes accessed | tf_op | source)
XLA Modules:
  0.0 319.1 jit_solution(9738041658170353303)
XLA Ops:
  7.2 1.5 pad_maximum_fusion.6
  8.8 1.1 copy.48
  10.0 1.9 multiply_reduce_fusion.1
  12.1 0.5 broadcast_multiply_fusion.2
  12.7 84.9 %all-gather.3.cloned.1.call-done = bf16[3584,1024]{1,0:T(8,128)(2,1)} async-done(((bf16[56,1024]{1,0:T(8,128)(2,1)}), bf16[3584,1024]{1,0:T(8,128)(2,1)}) %all-gather.3.cloned.1.call-update) | async-done | bytes 7340048 | tf_op jit(solution)/shard_map/all_gather | solution.py:91
  97.6 5.8 %fusion = f32[256,1024]{1,0:T(8,128)S(1)} fusion(bf16[3584,1024]{1,0:T(8,128)(2,1)} %all-gather.3.cloned.1.call-done, f32[3584]{0:T(1024)} %param.10, f32[256]{0:T(256)S(1)} %get-tuple-element.22, bf16[1,256,3584]{2,1,0:T(8,128)(2,1)} %param.6), kind=kOutput, calls=%fused_computation.4 | convolution fusion | flops 1882718208 | bytes 10238976 | tf_op jit(solution)/shard_map/dot_general | solution.py:92
  104.0 0.6 fusion.28
  104.6 2.0 collective-permute-start
  106.6 2.2 collective-permute-start.1
  109.4 1.3 collective-permute-done.1
  112.5 1.9 collective-permute-start.2
  115.0 1.9 collective-permute-start.3
  116.9 4.0 %collective-permute-done.2 = f32[256,1,256]{2,0,1:T(8,128)S(1)} collective-permute-done((f32[256,1,256]{2,0,1:T(8,128)S(1)}, f32[256,1,256]{2,0,1:T(8,128)S(1)}, u32[]{:S(2)}, u32[]{:S(2)}) %collective-permute-start.2) | collective-permute-done | bytes 262176 | tf_op jit(solution)/shard_map/ppermute | solution.py:24
  121.0 0.6 fusion.32
  121.7 2.1 collective-permute-done.3
  123.8 0.8 pad_maximum_fusion
  124.7 7.1 %fusion.45 = f32[256,3584]{1,0:T(8,128)} fusion(bf16[3584,1024]{1,0:T(8,128)(2,1)} %all-gather.3.cloned.1.call-done, bf16[256,256]{0,1:T(8,128)(2,1)S(1)} %fusion.36, bf16[256,256]{0,1:T(8,128)(2,1)S(1)} %copy.36, bf16[256,512]{0,1:T(8,128)(2,1)S(1)} %bitcast.105), kind=kOutput, calls=%fused_computation.91 | convolution fusion | flops 1880621056 | bytes 11534336 | tf_op jit(solution)/shard_map/dot_general | solution.py:146
  131.9 1.4 copy-done
  133.3 2.7 copy.22
  136.1 2.5 multiply_convert_fusion.1
  138.5 38.8 %all_to_all.16 = bf16[256,8,448]{0,2,1:T(8,128)(2,1)S(1)} all-to-all(bf16[256,8,448]{0,2,1:T(8,128)(2,1)S(1)} %multiply_convert_fusion.1), channel_id=1, replica_groups=mesh['seq'=8,'tensor'=4,'dp'=8] {'seq'}, dimensions={1} | all-to-all | bytes 3670016 | tf_op jit(solution)/shard_map/all_to_all | solution.py:135
  177.3 1.5 copy.49
  179.0 6.7 %multiply_reduce_fusion.2 = (f32[]{:T(128)}, f32[448,1024]{1,0:T(8,128)}) fusion(bf16[2048,448]{0,1:T(8,128)(2,1)} %bitcast.103, bf16[2048,1024]{0,1:T(8,128)(2,1)} %all-gather.5.cloned.1.call-done), kind=kOutput, calls=%fused_computation.5 | convolution fusion | flops 1879965696 | bytes 7864324 | tf_op jit(solution)/shard_map/dot_general | solution.py:136
  185.7 63.0 %psum.14 = f32[]{:T(128)} all-reduce(f32[]{:T(128)} %get-tuple-element.27), channel_id=1, replica_groups=mesh['seq'=8,'tensor'=4,'dp'=8] {'seq','tensor'}, use_global_device_ids=true, to_apply=%region_4.5 | all-reduce | flops 1 | bytes 8 | tf_op jit(solution)/shard_map/psum | solution.py:142
  249.4 3.0 broadcast_multiply_fusion.1
  252.5 2.3 convert_bitcast_fusion
  254.8 15.3 %all-reduce.2.cloned.1.call-done = f32[256,3584]{1,0:T(8,128)} async-done(((f32[256,3584]{1,0:T(8,128)}), f32[256,3584]{1,0:T(8,128)}) %all-reduce.2.cloned.1.call-update) | async-done | bytes 3670032 | tf_op jit(solution)/shard_map/psum | solution.py:151
  270.0 2.6 multiply_reduce_fusion
  272.7 2.2 fusion.15
  274.8 34.7 %reduce-scatter.2.cloned.1.call-done = f32[56,1024]{1,0:T(8,128)} async-done(((f32[448,1024]{1,0:T(8,128)}), f32[56,1024]{1,0:T(8,128)}) %reduce-scatter.2.cloned.1.call-update) | async-done | bytes 229392 | tf_op jit(solution)/shard_map/reduce_scatter | solution.py:145
  309.5 1.5 fusion.47
  311.0 1.6 slice.88
  (44 shorter events, 4.4 us)
Async XLA Ops:
  7.2 90.4 %all-gather.3.cloned.1.call-start = ((), (), s32[]{:S(2)}) async-start(), calls=%async_computation.2 | async-start | bytes 7454720 | tf_op jit(solution)/shard_map/all_gather | solution.py:91
  8.8 170.2 %all-gather.5.cloned.1.call-start = ((), (), s32[]{:S(2)}) async-start(), calls=%async_computation.3 | async-start | bytes 4718592 | tf_op jit(solution)/shard_map/all_gather | solution.py:138
  104.6 4.3 %collective-permute-start = (bf16[256,1,256]{2,0,1:T(8,128)(2,1)S(1)}, bf16[256,1,256]{2,0,1:T(8,128)(2,1)S(1)}, u32[]{:S(2)}, u32[]{:S(2)}) collective-permute-start(bf16[256,1,256]{2,0,1:T(8,128)(2,1)S(1)} %pad_maximum_fusion.5), channel_id=1, source_target_pairs={{0,32},{32,64},{64,96},{96,128},{128,160},{160,192},{192,224},{1,3... | collective-permute-start | bytes 393224 | tf_op jit(solution)/shard_map/ppermute | solution.py:24
  106.6 4.1 %collective-permute-start.1 = (bf16[256,1,256]{2,0,1:T(8,128)(2,1)S(1)}, bf16[256,1,256]{2,0,1:T(8,128)(2,1)S(1)}, u32[]{:S(2)}, u32[]{:S(2)}) collective-permute-start(bf16[256,1,256]{2,0,1:T(8,128)(2,1)S(1)} %fusion.35), channel_id=1, source_target_pairs={{0,32},{32,64},{64,96},{96,128},{128,160},{160,192},{192,224},{1,3... | collective-permute-start | bytes 393224 | tf_op jit(solution)/shard_map/ppermute | solution.py:24
  112.5 8.4 %collective-permute-start.2 = (f32[256,1,256]{2,0,1:T(8,128)S(1)}, f32[256,1,256]{2,0,1:T(8,128)S(1)}, u32[]{:S(2)}, u32[]{:S(2)}) collective-permute-start(f32[256,1,256]{2,0,1:T(8,128)S(1)} %slice.83), channel_id=1, source_target_pairs={{32,0},{64,32},{96,64},{128,96},{160,128},{192,160},{224,192},{33,... | collective-permute-start | bytes 786440 | tf_op jit(solution)/shard_map/ppermute | solution.py:24
  115.0 8.8 %collective-permute-start.3 = (f32[256,1,256]{0,2,1:T(8,128)S(1)}, f32[256,1,256]{0,2,1:T(8,128)S(1)}, u32[]{:S(2)}, u32[]{:S(2)}) collective-permute-start(f32[256,1,256]{0,2,1:T(8,128)S(1)} %slice.87), channel_id=1, source_target_pairs={{32,0},{64,32},{96,64},{128,96},{160,128},{192,160},{224,192},{33,... | collective-permute-start | bytes 786440 | tf_op jit(solution)/shard_map/ppermute | solution.py:24
  124.6 145.4 %all-reduce.2.cloned.1.call-start = ((), (), s32[]{:S(2)}) async-start(), calls=%async_computation.5 | async-start | bytes 7340032 | tf_op jit(solution)/shard_map/psum | solution.py:151
  131.8 1.5 copy-start
  131.8 4.2 %copy-start.1 = (f32[3584]{0:T(1024)S(1)}, f32[3584]{0:T(1024)}, u32[]{:S(2)}) copy-start(f32[3584]{0:T(1024)} %param.10) | copy-start | bytes 43012
  131.8 177.7 %reduce-scatter.2.cloned.1.call-start = ((), (), s32[]{:S(2)}) async-start(), calls=%async_computation.4 | async-start | bytes 2064384 | tf_op jit(solution)/shard_map/reduce_scatter | solution.py:145
Sparse Core Ops, SparseCore 0:
  11.3 86.2 all-gather.2
  124.8 54.1 all-gather.4
  181.3 88.6 all-reduce.1
  272.5 36.9 reduce-scatter.1
where the time goes:
time: 323 us; the launch traced here: 319 us
  waiting for transfers between devices  143 us (44%)
  blocking collectives  102 us (32%)
  matrix products  21.6 us (7%)
  other arithmetic  19.5 us (6%)
  between operations  14.8 us (5%)
  local copies, waits for them, and re-layouts  10.7 us (3%)
  starting transfers between devices  8.17 us (3%)
    all_gather x1, waiting for transfers between devices, local(): full_w = lax.all_gather(local_w, ('seq', 'dp'), axis=0, tiled=True)  84.9 us
    psum x1, blocking collectives, local(): square_sum = lax.psum(jnp.sum(grad_rows * grad_rows), ('seq', 'tensor'))  63 us
    all_to_all x1, blocking collectives, local(): lax.all_to_all(normed, 'seq', split_axis=1, concat_axis=0, tiled=True)  38.8 us
    reduce_scatter x1, waiting for transfers between devices, local(): lax.psum_scatter(factor * grad_rows, 'dp', scatter_dimension=0, tiled=True)  34.7 us
    psum x1, waiting for transfers between devices, local(): summed_grad = lax.psum(dnormed, 'tensor')  15.3 us
    ppermute x4, starting transfers between devices, shifted(): lax.ppermute(value, axis, [(source, source + steps) for source in range(l...  8 us
    ppermute x4, waiting for transfers between devices, shifted(): lax.ppermute(value, axis, [(source, source + steps) for source in range(l...  7.42 us
    dot_general x1, matrix products, local(): lax.dot_general(d_out, full_w, (((1,), (1,)), ((), ())), preferred_elemen...  7.1 us
  transfers between devices with their start and end apart: 8, of which 7 were waited for; matrix products, arithmetic and copies ran while one was open for 11% of the time, Pallas kernels for 0%

commit v1 on v0

v1 whole, which is shorter than its diff:
```python
import functools
import math

import jax
import jax.numpy as jnp
import numpy as np
from jax import lax
from jax.experimental import pallas as pl
from jax.experimental.pallas import tpu as pltpu
from jax.sharding import PartitionSpec as P

D = 3584
H = 8
KVH = 4
HD = 256
WINDOW = 256
SLAB = D // 4
ROWS = 56
TOK = 256

EPSILON = 1e-06
SOFTCAP = 50.0
CLIP_BOUND = 1.0
ROPE_BASE = 10000.0

F32 = jnp.float32
BF16 = jnp.bfloat16
VMEM = pl.BlockSpec(memory_space=pltpu.VMEM)
SMEM = pl.BlockSpec(memory_space=pltpu.SMEM)


def call(body, outs, place, *operands, scratch=()):
    return pl.pallas_call(
        body,
        out_shape=[jax.ShapeDtypeStruct(shape, kind) for shape, kind in outs],
        in_specs=[SMEM] + [VMEM] * len(operands),
        out_specs=[VMEM] * len(outs),
        scratch_shapes=list(scratch),
        compiler_params=pltpu.CompilerParams(vmem_limit_bytes=40 * 1024 * 1024),
    )(place, *operands)


def swap(value):
    return lax.ppermute(value, "seq", [(i, i ^ 1) for i in range(8)])


def from_x(value, steps):
    return lax.ppermute(value, "seq", [((i + 2 * steps) % 8, i) for i in range(8)])


def from_y(value, steps):
    return lax.ppermute(value, "tensor", [((i + steps) % 4, i) for i in range(4)])


def from_z(value, steps):
    return lax.ppermute(value, "dp", [((i + steps) % 8, i) for i in range(8)])


def mm(a, b, contract_a=1, contract_b=0):
    return lax.dot_general(
        a, b, (((contract_a,), (contract_b,)), ((), ())), preferred_element_type=F32
    )


def norm_body(place, inputs, gain, permute, normed, moved, inverse):
    rows = inputs[...].astype(F32)
    inv = lax.rsqrt(jnp.sum(rows * rows, -1, keepdims=True) * (1.0 / D) + EPSILON)
    inverse[...] = jnp.broadcast_to(inv, inverse.shape)
    for slab in range(4):
        part = mm(inputs[:, slab * SLAB : (slab + 1) * SLAB], permute[...])
        moved[slab] = part.astype(BF16)
        normed[slab] = (part * inv * gain[slab : slab + 1, :]).astype(BF16)


def stack_body(axis, count, rows, place, *refs):
    whole = refs[-1]
    for step in range(count):
        at = lax.rem(place[axis] + step, count)
        whole[pl.ds(pl.multiple_of(at * rows, 16), rows), :] = refs[step][...]


def columns_body(place, *refs):
    mine, theirs, whole = refs[:4], refs[4:8], refs[8]
    core = place[1]
    for step in range(4):
        a = mine[step][...].T
        b = theirs[step][...].T
        first = pl.multiple_of(core * TOK, TOK)
        second = pl.multiple_of((1 - core) * TOK, TOK)
        whole[step, :, pl.ds(first, TOK)] = a
        whole[step, :, pl.ds(second, TOK)] = b


def spin(value, cosine, sine, direction):
    first, second = value[:, :128], value[:, 128:]
    return jnp.concatenate(
        [first * cosine - direction * second * sine, second * cosine + direction * first * sine], -1
    )


def project_body(place, *refs):
    own, other, cos, sin, cos2, sin2 = refs[:6]
    slabs = refs[6:10]
    strips = refs[10:17]
    half_a, half_b = refs[17:19]
    query, pair, weights = refs[19:]
    x, core, z = place[0], place[1], place[3]
    for step in range(4):
        weights[lax.rem(x + step, 4), :, :HD] = slabs[step][...]

    def put(step, ref, groups, start):
        at = pl.multiple_of(lax.rem(z + step, 8) * 112, 16)
        for k, group in enumerate(groups):
            weights[group, pl.ds(at, 112), HD:] = ref[k * 112 : (k + 1) * 112, :]

    for strip, step in zip(strips, (0, 1, 2, 3, 7, 6, 5)):
        put(step, strip, (0, 1, 2, 3), 0)
    put(4, half_a, (0, 1), 0)
    put(4, half_b, (2, 3), 2)
    for rows, block in ((own, core), (other, 1 - core)):
        total = mm(rows[0], weights[0])
        for slab in range(1, 4):
            total += mm(rows[slab], weights[slab])
        at = pl.ds(pl.multiple_of(block * TOK, TOK), TOK)
        query[at, :] = spin(total[:, :HD], cos[at, :], sin[at, :], 1.0).astype(BF16)
        pair[at, :] = spin(total[:, HD:], cos2[at, :], sin2[at, :], 1.0).astype(BF16)


def attend_body(place, query, mine, theirs, mine_before, theirs_before, cot, cos, sin,
                dquery, keep, keep_before, send, send_before, keys, values):
    first_core = place[1] == 0
    for at, a, b in ((0, mine_before, theirs_before), (TOK, mine, theirs)):
        rows = a.shape[0]
        keys[at : at + rows, :] = jnp.where(first_core, a[...], b[...])
        values[at : at + rows, :] = jnp.where(first_core, b[...], a[...])
    scale = 1.0 / math.sqrt(HD)
    q_at = lax.broadcasted_iota(jnp.int32, (TOK, 2 * TOK), 0)
    k_at = lax.broadcasted_iota(jnp.int32, (TOK, 2 * TOK), 1)
    band = (k_at <= q_at + TOK) & (k_at > q_at)
    key_parts = []
    value_parts = []
    for block in range(2):
        here = slice(block * TOK, (block + 1) * TOK)
        seen = slice(block * TOK, (block + 2) * TOK)
        q, g = query[here, :], cot[here, :]
        k, v = keys[seen, :], values[seen, :]
        squash = jnp.tanh(mm(q, k, 1, 1) * (scale / SOFTCAP))
        allowed = band
        if block == 0:
            allowed = band & ((k_at >= TOK) | (place[0] > 0))
        terms = jnp.where(allowed, jnp.exp(SOFTCAP * squash), 0.0)
        probs = terms / jnp.sum(terms, -1, keepdims=True)
        dprobs = mm(g, v, 1, 1)
        value_parts.append(mm(probs.astype(BF16), g, 0, 0))
        delta = jnp.sum(probs * dprobs, -1, keepdims=True)
        dlogits = (probs * (dprobs - delta) * (1.0 - squash * squash) * scale).astype(BF16)
        dq = mm(dlogits, k)
        dquery[here, :] = spin(dq, cos[here, :], sin[here, :], -1.0).astype(BF16)
        key_parts.append(mm(dlogits, q, 0, 0))

    def place_out(dk, dv, keep_at, send_at):
        keep_at[...] = jnp.where(first_core, dk, dv)
        send_at[...] = jnp.where(first_core, dv, dk).astype(BF16)

    place_out(key_parts[0][:TOK], value_parts[0][:TOK], keep_before, send_before)
    place_out(
        key_parts[0][TOK:] + key_parts[1][:TOK],
        value_parts[0][TOK:] + value_parts[1][:TOK],
        keep.at[:TOK, :],
        send.at[:TOK, :],
    )
    place_out(key_parts[1][TOK:], value_parts[1][TOK:], keep.at[TOK:, :], send.at[TOK:, :])


def halo_body(place, keep_before, got_before, out):
    out[...] = (keep_before[...] + got_before[...].astype(F32)).astype(BF16)


def pair_body(place, keep, got, back, cos2, sin2, dpair):
    for block in range(2):
        here = slice(block * TOK, (block + 1) * TOK)
        total = keep[here, :] + got[here, :].astype(F32)
        if block == 1:
            total += back[...].astype(F32)
        dpair[here, :] = spin(total, cos2[here, :], sin2[here, :], -1.0).astype(BF16)


def dnormed_body(place, dquery, dpair, weights, own, other, keep, send, keep_sum, send_sum):
    core = place[1]
    for rows, block, out, sums in (
        (other, 1 - core, send, send_sum),
        (own, core, keep, keep_sum),
    ):
        at = pl.ds(pl.multiple_of(block * TOK, TOK), TOK)
        dq, dp = dquery[at, :], dpair[at, :]
        total = jnp.zeros((TOK, 1), F32)
        for slab in range(4):
            part = mm(dq, weights[slab, :, :HD], 1, 1) + mm(dp, weights[slab, :, HD:], 1, 1)
            total += jnp.sum(part * rows[slab].astype(F32), -1, keepdims=True)
            out[slab] = part.astype(BF16)
        sums[...] = jnp.broadcast_to(total, sums.shape)


def split_body(place, keep, got, keep_sum, got_sum, own, own_sum, *messages):
    y = place[2]
    total = keep_sum[...] + got_sum[...]
    own_sum[...] = total
    high = total.astype(BF16)
    rest = total - high.astype(F32)
    middle = rest.astype(BF16)
    low = (rest - middle.astype(F32)).astype(BF16)
    lane = lax.broadcasted_iota(jnp.int32, total.shape, 1)
    zero = jnp.zeros_like(total)
    coded = jnp.where(
        lane == 0,
        high.astype(F32),
        jnp.where(lane == 1, middle.astype(F32), jnp.where(lane == 2, low.astype(F32), zero)),
    ).astype(BF16)
    own[...] = keep[y].astype(F32) + got[y].astype(F32)
    for step, message in enumerate(messages):
        at = lax.rem(y + 4 - (step + 1), 4)
        message[:, :SLAB] = (keep[at].astype(F32) + got[at].astype(F32)).astype(BF16)
        message[:, SLAB:] = coded


def input_body(place, own, own_sum, m1, m2, m3, moved, inverse, gain, permute, out):
    total = own[...]
    sums = own_sum[:, :1]
    for message in (m1, m2, m3):
        total += message[:, :SLAB].astype(F32)
        sums += jnp.sum(message[:, SLAB:].astype(F32), -1, keepdims=True)
    inv = inverse[:, :1]
    y = place[2]
    rows = moved[y].astype(F32)
    grad = inv * (gain[pl.ds(y, 1), :] * total) - rows * ((inv * inv) * (sums * (1.0 / D)))
    out[0] = mm(grad.astype(BF16), permute[...], 1, 1).astype(BF16)


def weights_body(place, columns, d0, d1, d2, d3, *refs):
    chunks, squares, total = refs[:8], refs[8], refs[9]
    z = place[3]
    acc = mm(columns[0], d0[...])
    for step, d in ((1, d1), (2, d2), (3, d3)):
        acc += mm(columns[step], d[...])
    total[...] = acc
    squares[...] = jnp.full(squares.shape, jnp.sum(acc * acc), F32)
    for step in range(8):
        at = lax.rem(z + 8 - step, 8)
        chunks[step][...] = total[pl.ds(pl.multiple_of(at * 112, 16), 112), :].astype(BF16)


def clip_body(place, *refs):
    halves, squares, keep, send = (refs[:8], refs[8:16]), refs[16:24], refs[24], refs[25]
    core = place[1]
    factors = []
    for total in squares:
        rms = jnp.sqrt(total[...] * (1.0 / (D * (H + 2 * KVH) * HD)) + EPSILON)
        factors.append((CLIP_BOUND / jnp.maximum(rms, CLIP_BOUND))[:1, :1])
    for half in range(2):
        total = halves[half][0][...].astype(F32) * factors[0]
        for step in range(1, 8):
            total += halves[half][step][...].astype(F32) * factors[step]
        top, bottom = total[:ROWS], total[ROWS:]
        at = slice(half * HD, (half + 1) * HD)
        keep[:, at] = jnp.where(core == 0, top, bottom)
        send[:, at] = jnp.where(core == 0, bottom, top)


def out_body(place, keep, got, grad_query, grad_key, grad_value):
    first = place[1] == 0
    mine, theirs = keep[...], got[...]
    zero = jnp.where(first, mine, theirs)
    one = jnp.where(first, theirs, mine)
    grad_query[:, :HD] = zero[:, :HD]
    grad_query[:, HD:] = one[:, :HD]
    grad_key[...] = zero[:, HD:]
    grad_value[...] = one[:, HD:]


def local(inputs, w_query, w_key, w_value, norm_gain, attn_grad):
    seq = lax.axis_index("seq").astype(jnp.int32)
    x, core = seq // 2, seq % 2
    y = lax.axis_index("tensor").astype(jnp.int32)
    z = lax.axis_index("dp").astype(jnp.int32)
    place = jnp.stack([x, core, y, z])
    first = core == 0

    low, high = w_query[:, :HD], w_query[:, HD:]
    mine = jnp.concatenate([jnp.where(first, low, high), jnp.where(first, w_key, w_value)], 1)
    theirs = jnp.concatenate([jnp.where(first, high, low), jnp.where(first, w_value, w_key)], 1)
    got = swap(theirs)
    block = jnp.concatenate([jnp.where(first, mine, got), jnp.where(first, got, mine)], 0)
    block_q, block_p = block[:, :HD], block[:, HD:]
    (strip,) = call(
        functools.partial(stack_body, 0, 4, 112),
        [((448, HD), BF16)],
        place,
        *[block_p if step == 0 else from_x(block_p, step) for step in range(4)],
    )
    ups, downs = [strip], [strip]
    for _ in range(3):
        ups.append(from_z(ups[-1], 1))
        downs.append(from_z(downs[-1], -1))
    half_a = from_z(ups[-1][:224], 1)
    half_b = from_z(downs[-1][224:], -1)
    strips = ups + downs[1:]
    (slab,) = call(
        functools.partial(stack_body, 3, 8, 112),
        [((SLAB, HD), BF16)],
        place,
        *[block_q if step == 0 else from_z(block_q, step) for step in range(8)],
    )
    slabs = [slab if step == 0 else from_x(slab, step) for step in range(4)]

    index = np.arange(SLAB)
    natural = (index % 112) // ROWS * 448 + index // 112 * ROWS + index % ROWS
    permute = (
        lax.broadcasted_iota(jnp.int32, (SLAB, SLAB), 0) == jnp.asarray(natural, jnp.int32)[None, :]
    ).astype(BF16)
    gain = norm_gain.reshape(4, 2, 8, ROWS).transpose(0, 2, 1, 3).reshape(4, SLAB)
    normed, moved, inverse = call(
        norm_body,
        [((4, TOK, SLAB), BF16), ((4, TOK, SLAB), BF16), ((TOK, 128), F32)],
        place,
        inputs[0],
        gain,
        permute,
    )
    normed_other = swap(normed)
    cot_low, cot_high = attn_grad[0][:, :HD], attn_grad[0][:, HD:]
    cot_mine = jnp.where(first, cot_low, cot_high)
    cot_got = swap(jnp.where(first, cot_high, cot_low))
    cot = jnp.concatenate(
        [jnp.where(first, cot_mine, cot_got), jnp.where(first, cot_got, cot_mine)], 0
    )

    positions = x * (2 * TOK) + jnp.arange(2 * TOK, dtype=jnp.int32)
    frequency = ROPE_BASE ** (-2.0 * jnp.arange(HD // 2).astype(F32) / HD)
    phases = positions.astype(F32)[:, None] * frequency[None, :]
    cos, sin = jnp.cos(phases), jnp.sin(phases)
    cos2, sin2 = jnp.where(first, cos, 1.0), jnp.where(first, sin, 0.0)

    query, pair, weights = call(
        project_body,
        [((2 * TOK, HD), BF16), ((2 * TOK, HD), BF16), ((4, SLAB, 2 * HD), BF16)],
        place,
        normed,
        normed_other,
        cos,
        sin,
        cos2,
        sin2,
        *slabs,
        *strips,
        half_a,
        half_b,
    )

    columns_mine = [lax.dynamic_index_in_dim(normed, x, 0, False)] + [
        from_x(lax.dynamic_index_in_dim(normed, (x + 4 - step) % 4, 0, False), step)
        for step in range(1, 4)
    ]
    columns_other = [lax.dynamic_index_in_dim(normed_other, x, 0, False)] + [
        swap(columns_mine[step]) for step in range(1, 4)
    ]
    (columns,) = call(
        columns_body, [((4, SLAB, 2 * TOK), BF16)], place, *columns_mine, *columns_other
    )

    pair_other = swap(pair)
    before = from_x(pair[TOK:], -1)
    before_other = lax.ppermute(
        pair[TOK:], "seq", [(i, ((i ^ 1) + 2) % 8) for i in range(8)]
    )
    dquery, keep, keep_before, send, send_before = call(
        attend_body,
        [
            ((2 * TOK, HD), BF16),
            ((2 * TOK, HD), F32),
            ((TOK, HD), F32),
            ((2 * TOK, HD), BF16),
            ((TOK, HD), BF16),
        ],
        place,
        query,
        pair,
        pair_other,
        before,
        before_other,
        cot,
        cos,
        sin,
        scratch=[pltpu.VMEM((3 * TOK, HD), BF16), pltpu.VMEM((3 * TOK, HD), BF16)],
    )
    got_before = swap(send_before)
    got = swap(send)
    dquery_all = [dquery] + [from_x(dquery, step) for step in range(1, 4)]
    (back,) = call(halo_body, [((TOK, HD), BF16)], place, keep_before, got_before)
    back = from_x(back, 1)
    (dpair,) = call(pair_body, [((2 * TOK, HD), BF16)], place, keep, got, back, cos2, sin2)
    dpair_all = [dpair] + [from_x(dpair, step) for step in range(1, 4)]

    keep_in, send_in, keep_sum, send_sum = call(
        dnormed_body,
        [
            ((4, TOK, SLAB), BF16),
            ((4, TOK, SLAB), BF16),
            ((TOK, 128), F32),
            ((TOK, 128), F32),
        ],
        place,
        dquery,
        dpair,
        weights,
        normed,
        normed_other,
    )
    got_in, got_sum = swap(send_in), swap(send_sum)
    own, own_sum, *messages = call(
        split_body,
        [((TOK, SLAB), F32), ((TOK, 128), F32)] + [((TOK, SLAB + 128), BF16)] * 3,
        place,
        keep_in,
        got_in,
        keep_sum,
        got_sum,
    )
    arrived = [from_y(message, step + 1) for step, message in enumerate(messages)]
    (input_grad,) = call(
        input_body,
        [((1, TOK, SLAB), BF16)],
        place,
        own,
        own_sum,
        *arrived,
        moved,
        inverse,
        gain,
        permute,
    )

    halves = []
    square = 0.0
    for parts in (dquery_all, dpair_all):
        *chunks, squares = call(
            weights_body,
            [((112, HD), BF16)] * 8 + [((8, 128), F32)],
            place,
            columns,
            *parts,
            scratch=[pltpu.VMEM((SLAB, HD), F32)],
        )
        halves += [chunk if step == 0 else from_z(chunk, step) for step, chunk in enumerate(chunks)]
        square = square + squares
    square = square + swap(square)
    square = square + from_x(square, 1) + from_x(square, 2) + from_x(square, 3)
    square = square + from_y(square, 1) + from_y(square, 2) + from_y(square, 3)
    squares = [square if step == 0 else from_z(square, step) for step in range(8)]
    keep_out, send_out = call(
        clip_body,
        [((ROWS, 2 * HD), F32), ((ROWS, 2 * HD), F32)],
        place,
        *halves,
        *squares,
    )
    got_out = swap(send_out)
    grad_query, grad_key, grad_value = call(
        out_body,
        [((ROWS, 2 * HD), F32), ((ROWS, HD), F32), ((ROWS, HD), F32)],
        place,
        keep_out,
        got_out,
    )
    return grad_query, grad_key, grad_value, input_grad


def solution(mesh):
    return jax.shard_map(
        local,
        mesh=mesh,
        in_specs=(
            P("dp", "seq", None),
            P(("seq", "dp"), "tensor"),
            P(("seq", "dp"), "tensor"),
            P(("seq", "dp"), "tensor"),
            P(),
            P("dp", "seq", "tensor"),
        ),
        out_specs=(
            P(("seq", "dp"), "tensor"),
            P(("seq", "dp"), "tensor"),
            P(("seq", "dp"), "tensor"),
            P("dp", "seq", "tensor"),
        ),
        check_vma=False,
    )
```

time: 323 us -> 295 us (0.913)
  the two profiles are of different devices: /device:TPU:1 before, /device:TPU:11 now
where the time goes in v1:
time: 295 us; the launch traced here: 289 us
  starting transfers between devices  147 us (50%)
  waiting for transfers between devices  88.9 us (30%)
  Pallas kernels  30.8 us (10%)
  local copies, waits for them, and re-layouts  17.1 us (6%)
  other arithmetic  4.21 us (1%)
    ppermute x36, starting transfers between devices, from_z(): return lax.ppermute(value, 'dp', [((i + steps) % 8, i) for i in range(8)])  62.6 us
    ppermute x36, waiting for transfers between devices, from_z(): return lax.ppermute(value, 'dp', [((i + steps) % 8, i) for i in range(8)])  43.6 us
    ppermute x13, starting transfers between devices, swap(): return lax.ppermute(value, 'seq', [(i, i ^ 1) for i in range(8)])  38.1 us
    ppermute x20, waiting for transfers between devices, from_x(): lax.ppermute(value, 'seq', [((i + 2 * steps) % 8, i) for i in range(8)])  36 us
    pallas_call x15, Pallas kernels, call(): pl.pallas_call(body, out_shape=[jax.ShapeDtypeStruct(shape, kind) for sha...  30.8 us
    ppermute x20, starting transfers between devices, from_x(): lax.ppermute(value, 'seq', [((i + 2 * steps) % 8, i) for i in range(8)])  27.8 us
    unnamed x62, local copies, waits for them, and re-layouts  14 us
    ppermute x1, starting transfers between devices, local(): lax.ppermute(pair[TOK:], 'seq', [(i, ((i ^ 1) + 2) % 8) for i in range(8)])  11.5 us
  transfers between devices with their start and end apart: 76, of which 36 were waited for; matrix products, arithmetic and copies ran while one was open for 2% of the time, Pallas kernels for 6%

profile of v1, /device:TPU:11, one launch (start us, length us, event | category | flops | bytes accessed | tf_op | source)
XLA Modules:
  0.0 289.3 jit_solution(16621287295095143488)
XLA Ops:
  4.5 3.2 %shard_map.102 = (bf16[4,256,896]{2,1,0:T(8,128)(2,1)S(1)}, bf16[4,256,896]{2,1,0:T(8,128)(2,1)S(1)}, f32[256,128]{1,0:T(8,128)S(1)}) custom-call(s32[4]{0:T(128)S(1)} %pad_add_fusion.place, bf16[256,3584]{1,0:T(8,128)(2,1)S(1)} %bitcast.17, f32[4,896]{1,0:T(4,128)S(1)} %reshape.27.gain, bf16[896,896]{1,0:T(8,128)(2,1)S(1)} %fusion.permute), custom_call_target="tpu_custom_call" | custom-call | tf_op jit(solution)/shard_map/pallas_call | solution.py:33
  20.3 5.7 %collective-permute-start.21 = (bf16[448,256]{1,0:T(8,128)(2,1)S(1)}, bf16[448,256]{1,0:T(8,128)(2,1)S(1)}, u32[]{:S(2)}, u32[]{:S(2)}) collective-permute-start(bf16[448,256]{1,0:T(8,128)(2,1)S(1)} %shard_map.105.refs_10_), channel_id=1, source_target_pairs={{1,0},{2,1},{3,2},{4,3},{5,4},{6,5},{7,6},{0,7},{9,8},{10,9},{11,1... | collective-permute-start | bytes 688136 | tf_op jit(solution)/shard_map/ppermute | solution.py:56
  29.1 3.4 %collective-permute-start.22 = (bf16[448,256]{1,0:T(8,128)(2,1)S(1)}, bf16[448,256]{1,0:T(8,128)(2,1)}, u32[]{:S(2)}, u32[]{:S(2)}) collective-permute-start(bf16[448,256]{1,0:T(8,128)(2,1)S(1)} %collective-permute-done.21.refs_11_), channel_id=1, source_target_pairs={{1,0},{2,1},{3,2},{4,3},{5,4},{6,5},{7,6},{0,7},{9,8},{10,9},{11,1... | collective-permute-start | bytes 688136 | tf_op jit(solution)/shard_map/ppermute | solution.py:56
  35.5 3.6 %collective-permute-done.10.refs_3_ = bf16[112,256]{1,0:T(8,128)(2,1)S(1)} collective-permute-done((bf16[112,256]{1,0:T(8,128)(2,1)S(1)}, bf16[112,256]{1,0:T(8,128)(2,1)S(1)}, u32[]{:S(2)}, u32[]{:S(2)}) %collective-permute-start.10) | collective-permute-done | bytes 57376 | tf_op jit(solution)/shard_map/ppermute | solution.py:56
  40.7 5.6 %collective-permute-start.13 = (bf16[112,256]{1,0:T(8,128)(2,1)S(1)}, bf16[112,256]{1,0:T(8,128)(2,1)S(1)}, u32[]{:S(2)}, u32[]{:S(2)}) collective-permute-start(bf16[112,256]{1,0:T(8,128)(2,1)S(1)} %get-tuple-element.97.refs_0_), channel_id=1, source_target_pairs={{6,0},{7,1},{0,2},{1,3},{2,4},{3,5},{4,6},{5,7},{14,8},{15,9},{8,1... | collective-permute-start | bytes 172040 | tf_op jit(solution)/shard_map/ppermute | solution.py:56
  47.9 2.7 collective-permute-start.8
  52.6 3.1 %collective-permute-start.9 = (bf16[112,256]{1,0:T(8,128)(2,1)S(1)}, bf16[112,256]{1,0:T(8,128)(2,1)S(1)}, u32[]{:S(2)}, u32[]{:S(2)}) collective-permute-start(bf16[112,256]{1,0:T(8,128)(2,1)S(1)} %get-tuple-element.97.refs_0_), channel_id=1, source_target_pairs={{2,0},{3,1},{4,2},{5,3},{6,4},{7,5},{0,6},{1,7},{10,8},{11,9},{12,... | collective-permute-start | bytes 172040 | tf_op jit(solution)/shard_map/ppermute | solution.py:56
  55.6 2.7 collective-permute-start.23
  65.5 4.4 %collective-permute-done.26.refs_16_ = bf16[448,256]{1,0:T(8,128)(2,1)S(1)} collective-permute-done((bf16[448,256]{1,0:T(8,128)(2,1)}, bf16[448,256]{1,0:T(8,128)(2,1)S(1)}, u32[]{:S(2)}, u32[]{:S(2)}) %collective-permute-start.26) | collective-permute-done | bytes 229408 | tf_op jit(solution)/shard_map/ppermute | solution.py:56
  69.9 7.9 %collective-permute-start.32 = (bf16[256,256]{1,0:T(8,128)(2,1)S(1)}, bf16[256,256]{1,0:T(8,128)(2,1)S(1)}, u32[]{:S(2)}, u32[]{:S(2)}) collective-permute-start(bf16[256,256]{1,0:T(8,128)(2,1)S(1)} %broadcast_select_fusion.4), channel_id=1, source_target_pairs={{0,32},{32,0},{64,96},{96,64},{128,160},{160,128},{192,224},{224,1... | collective-permute-start | bytes 393224 | tf_op jit(solution)/shard_map/ppermute | solution.py:44
  83.5 4.8 %shard_map.106 = (bf16[512,256]{1,0:T(8,128)(2,1)S(1)}, bf16[512,256]{1,0:T(8,128)(2,1)S(1)}, bf16[4,896,512]{2,1,0:T(8,128)(2,1)S(1)}) custom-call(s32[4]{0:T(128)S(1)} %pad_add_fusion.place, bf16[4,256,896]{2,1,0:T(8,128)(2,1)S(1)} %get-tuple-element.47.refs_0_.own, bf16[4,256,896]{2,1,0:T(8,128)(2,1)} %collective-permute-done.3.refs_1_.other, ...), custom_call_target="tpu_custom_call" | custom-call | tf_op jit(solution)/shard_map/pallas_call | solution.py:33
  88.4 6.8 %collective-permute-start.29 = (bf16[512,256]{1,0:T(8,128)(2,1)S(1)}, bf16[512,256]{1,0:T(8,128)(2,1)S(1)}, u32[]{:S(2)}, u32[]{:S(2)}) collective-permute-start(bf16[512,256]{1,0:T(8,128)(2,1)S(1)} %get-tuple-element.49.mine), channel_id=1, source_target_pairs={{0,32},{32,0},{64,96},{96,64},{128,160},{160,128},{192,224},{224,1... | collective-permute-start | bytes 786440 | tf_op jit(solution)/shard_map/ppermute | solution.py:44
  95.2 11.5 %collective-permute-start.31 = (bf16[256,256]{1,0:T(8,128)(2,1)S(1)}, bf16[256,256]{1,0:T(8,128)(2,1)S(1)}, u32[]{:S(2)}, u32[]{:S(2)}) collective-permute-start(bf16[256,256]{1,0:T(8,128)(2,1)S(1)} %slice.34), channel_id=1, source_target_pairs={{0,96},{32,64},{64,160},{96,128},{128,224},{160,192},{192,32},{224... | collective-permute-start | bytes 393224 | tf_op jit(solution)/shard_map/ppermute | solution.py:372
  106.7 2.9 %collective-permute-done.31.theirs_before = bf16[256,256]{1,0:T(8,128)(2,1)S(1)} collective-permute-done((bf16[256,256]{1,0:T(8,128)(2,1)S(1)}, bf16[256,256]{1,0:T(8,128)(2,1)S(1)}, u32[]{:S(2)}, u32[]{:S(2)}) %collective-permute-start.31) | collective-permute-done | bytes 131104 | tf_op jit(solution)/shard_map/ppermute | solution.py:372
  109.7 2.8 shard_map.107
  118.8 3.9 %collective-permute-done.45.back = bf16[256,256]{1,0:T(8,128)(2,1)} collective-permute-done((bf16[256,256]{1,0:T(8,128)(2,1)}, bf16[256,256]{1,0:T(8,128)(2,1)}, u32[]{:S(2)}, u32[]{:S(2)}) %collective-permute-start.45) | collective-permute-done | bytes 131104 | tf_op jit(solution)/shard_map/ppermute | solution.py:48
  129.0 4.1 %shard_map.114 = (bf16[4,256,896]{2,1,0:T(8,128)(2,1)S(1)}, bf16[4,256,896]{2,1,0:T(8,128)(2,1)}, f32[256,128]{1,0:T(8,128)S(1)}, f32[256,128]{1,0:T(8,128)S(1)}) custom-call(s32[4]{0:T(128)S(1)} %pad_add_fusion.place, bf16[512,256]{1,0:T(8,128)(2,1)S(1)} %copy-done.14, bf16[512,256]{1,0:T(8,128)(2,1)S(1)} %shard_map.110.d0.dpair, ...), custom_call_target="tpu_custom_call" | custom-call | tf_op jit(solution)/shard_map/pallas_call | solution.py:33
  141.3 7.6 %collective-permute-done.refs_1_ = bf16[256,896]{1,0:T(8,128)(2,1)S(1)} collective-permute-done((bf16[256,896]{1,0:T(8,128)(2,1)S(1)}, bf16[256,896]{1,0:T(8,128)(2,1)S(1)}, u32[]{:S(2)}, u32[]{:S(2)}) %collective-permute-start) | collective-permute-done | bytes 458784 | tf_op jit(solution)/shard_map/ppermute | solution.py:48
  149.7 10.2 %collective-permute-done.1.refs_2_ = bf16[256,896]{1,0:T(8,128)(2,1)S(1)} collective-permute-done((bf16[256,896]{1,0:T(8,128)(2,1)S(1)}, bf16[256,896]{1,0:T(8,128)(2,1)S(1)}, u32[]{:S(2)}, u32[]{:S(2)}) %collective-permute-start.1) | collective-permute-done | bytes 458784 | tf_op jit(solution)/shard_map/ppermute | solution.py:48
  161.5 2.6 collective-permute-start.33
  166.5 3.3 %collective-permute-done.33.d1 = bf16[512,256]{1,0:T(8,128)(2,1)S(1)} collective-permute-done((bf16[512,256]{1,0:T(8,128)(2,1)S(1)}, bf16[512,256]{1,0:T(8,128)(2,1)S(1)}, u32[]{:S(2)}, u32[]{:S(2)}) %collective-permute-start.33) | collective-permute-done | bytes 262176 | tf_op jit(solution)/shard_map/ppermute | solution.py:48
  169.8 3.1 %collective-permute-start.47 = (bf16[512,256]{1,0:T(8,128)(2,1)S(1)}, bf16[512,256]{1,0:T(8,128)(2,1)S(1)}, u32[]{:S(2)}, u32[]{:S(2)}) collective-permute-start(bf16[512,256]{1,0:T(8,128)(2,1)S(1)} %copy-done.3), channel_id=1, source_target_pairs={{128,0},{160,32},{192,64},{224,96},{0,128},{32,160},{64,192},{96,2... | collective-permute-start | bytes 786440 | tf_op jit(solution)/shard_map/ppermute | solution.py:48
  173.0 3.0 %collective-permute-done.34.d2 = bf16[512,256]{1,0:T(8,128)(2,1)S(1)} collective-permute-done((bf16[512,256]{1,0:T(8,128)(2,1)S(1)}, bf16[512,256]{1,0:T(8,128)(2,1)S(1)}, u32[]{:S(2)}, u32[]{:S(2)}) %collective-permute-start.34) | collective-permute-done | bytes 262176 | tf_op jit(solution)/shard_map/ppermute | solution.py:48
  182.6 4.6 %collective-permute-done.47.d2 = bf16[512,256]{1,0:T(8,128)(2,1)S(1)} collective-permute-done((bf16[512,256]{1,0:T(8,128)(2,1)S(1)}, bf16[512,256]{1,0:T(8,128)(2,1)S(1)}, u32[]{:S(2)}, u32[]{:S(2)}) %collective-permute-start.47) | collective-permute-done | bytes 262176 | tf_op jit(solution)/shard_map/ppermute | solution.py:48
  199.0 2.7 collective-permute-start.40
  212.8 2.7 collective-permute-start.49
  222.5 2.6 collective-permute-done.64.refs_18_
  226.7 2.7 collective-permute-done.65.refs_19_
  229.4 2.7 collective-permute-start.66
  232.1 3.6 %collective-permute-done.66.refs_20_ = f32[8,128]{1,0:T(8,128)S(1)} collective-permute-done((f32[8,128]{1,0:T(8,128)S(1)}, f32[8,128]{1,0:T(8,128)S(1)}, u32[]{:S(2)}, u32[]{:S(2)}) %collective-permute-start.66) | collective-permute-done | bytes 4128 | tf_op jit(solution)/shard_map/ppermute | solution.py:56
  235.8 3.2 %collective-permute-start.67 = (f32[8,128]{1,0:T(8,128)S(1)}, f32[8,128]{1,0:T(8,128)S(1)}, u32[]{:S(2)}, u32[]{:S(2)}) collective-permute-start(f32[8,128]{1,0:T(8,128)S(1)} %add_add_fusion.refs_16_), channel_id=1, source_target_pairs={{5,0},{6,1},{7,2},{0,3},{1,4},{2,5},{3,6},{4,7},{13,8},{14,9},{15,... | collective-permute-start | bytes 12296 | tf_op jit(solution)/shard_map/ppermute | solution.py:56
  269.0 15.5 %collective-permute-start.70 = (f32[56,512]{1,0:T(8,128)S(1)}, f32[56,512]{1,0:T(8,128)S(1)}, u32[]{:S(2)}, u32[]{:S(2)}) collective-permute-start(f32[56,512]{1,0:T(8,128)S(1)} %get-tuple-element.74), channel_id=1, source_target_pairs={{0,32},{32,0},{64,96},{96,64},{128,160},{160,128},{192,224},{224,1... | collective-permute-start | bytes 344072 | tf_op jit(solution)/shard_map/ppermute | solution.py:44
  (221 shorter events, 138.6 us)
Async XLA Ops:
  9.6 73.9 %collective-permute-start.3 = (bf16[4,256,896]{2,1,0:T(8,128)(2,1)S(1)}, bf16[4,256,896]{2,1,0:T(8,128)(2,1)}, u32[]{:S(2)}, u32[]{:S(2)}) collective-permute-start(bf16[4,256,896]{2,1,0:T(8,128)(2,1)S(1)} %get-tuple-element.47.refs_0_.own), channel_id=1, source_target_pairs={{0,32},{32,0},{64,96},{96,64},{128,160},{160,128},{192,224},{224,1... | collective-permute-start | bytes 5505032 | tf_op jit(solution)/shard_map/ppermute | solution.py:44
  25.9 29.7 %collective-permute-start.24 = (bf16[448,256]{1,0:T(8,128)(2,1)S(1)}, bf16[448,256]{1,0:T(8,128)(2,1)}, u32[]{:S(2)}, u32[]{:S(2)}) collective-permute-start(bf16[448,256]{1,0:T(8,128)(2,1)S(1)} %shard_map.105.refs_10_), channel_id=1, source_target_pairs={{7,0},{0,1},{1,2},{2,3},{3,4},{4,5},{5,6},{6,7},{15,8},{8,9},{9,10... | collective-permute-start | bytes 688136 | tf_op jit(solution)/shard_map/ppermute | solution.py:56
  29.1 26.5 %collective-permute-start.22 = (bf16[448,256]{1,0:T(8,128)(2,1)S(1)}, bf16[448,256]{1,0:T(8,128)(2,1)}, u32[]{:S(2)}, u32[]{:S(2)}) collective-permute-start(bf16[448,256]{1,0:T(8,128)(2,1)S(1)} %collective-permute-done.21.refs_11_), channel_id=1, source_target_pairs={{1,0},{2,1},{3,2},{4,3},{5,4},{6,5},{7,6},{0,7},{9,8},{10,9},{11,1... | collective-permute-start | bytes 688136 | tf_op jit(solution)/shard_map/ppermute | solution.py:56
  47.9 10.4 %collective-permute-start.8 = (bf16[112,256]{1,0:T(8,128)(2,1)S(1)}, bf16[112,256]{1,0:T(8,128)(2,1)S(1)}, u32[]{:S(2)}, u32[]{:S(2)}) collective-permute-start(bf16[112,256]{1,0:T(8,128)(2,1)S(1)} %get-tuple-element.97.refs_0_), channel_id=1, source_target_pairs={{1,0},{2,1},{3,2},{4,3},{5,4},{6,5},{7,6},{0,7},{9,8},{10,9},{11,1... | collective-permute-start | bytes 172040 | tf_op jit(solution)/shard_map/ppermute | solution.py:56
  59.6 18.2 %collective-permute-start.15 = (bf16[896,256]{1,0:T(8,128)(2,1)}, bf16[896,256]{1,0:T(8,128)(2,1)}, u32[]{:S(2)}, u32[]{:S(2)}) collective-permute-start(bf16[896,256]{1,0:T(8,128)(2,1)} %shard_map.104.refs_6_), channel_id=1, source_target_pairs={{64,0},{96,32},{128,64},{160,96},{192,128},{224,160},{0,192},{32,2... | collective-permute-start | bytes 1376264 | tf_op jit(solution)/shard_map/ppermute | solution.py:48
  62.0 16.4 %collective-permute-start.16 = (bf16[896,256]{1,0:T(8,128)(2,1)}, bf16[896,256]{1,0:T(8,128)(2,1)}, u32[]{:S(2)}, u32[]{:S(2)}) collective-permute-start(bf16[896,256]{1,0:T(8,128)(2,1)} %shard_map.104.refs_6_), channel_id=1, source_target_pairs={{128,0},{160,32},{192,64},{224,96},{0,128},{32,160},{64,192},{96,2... | collective-permute-start | bytes 1376264 | tf_op jit(solution)/shard_map/ppermute | solution.py:48
  62.5 18.6 %collective-permute-start.17 = (bf16[896,256]{1,0:T(8,128)(2,1)}, bf16[896,256]{1,0:T(8,128)(2,1)S(1)}, u32[]{:S(2)}, u32[]{:S(2)}) collective-permute-start(bf16[896,256]{1,0:T(8,128)(2,1)} %shard_map.104.refs_6_), channel_id=1, source_target_pairs={{192,0},{224,32},{0,64},{32,96},{64,128},{96,160},{128,192},{160,2... | collective-permute-start | bytes 1376264 | tf_op jit(solution)/shard_map/ppermute | solution.py:48
  69.9 36.7 %collective-permute-start.32 = (bf16[256,256]{1,0:T(8,128)(2,1)S(1)}, bf16[256,256]{1,0:T(8,128)(2,1)S(1)}, u32[]{:S(2)}, u32[]{:S(2)}) collective-permute-start(bf16[256,256]{1,0:T(8,128)(2,1)S(1)} %broadcast_select_fusion.4), channel_id=1, source_target_pairs={{0,32},{32,0},{64,96},{96,64},{128,160},{160,128},{192,224},{224,1... | collective-permute-start | bytes 393224 | tf_op jit(solution)/shard_map/ppermute | solution.py:44
  88.4 21.3 %collective-permute-start.29 = (bf16[512,256]{1,0:T(8,128)(2,1)S(1)}, bf16[512,256]{1,0:T(8,128)(2,1)S(1)}, u32[]{:S(2)}, u32[]{:S(2)}) collective-permute-start(bf16[512,256]{1,0:T(8,128)(2,1)S(1)} %get-tuple-element.49.mine), channel_id=1, source_target_pairs={{0,32},{32,0},{64,96},{96,64},{128,160},{160,128},{192,224},{224,1... | collective-permute-start | bytes 786440 | tf_op jit(solution)/shard_map/ppermute | solution.py:44
  95.1 11.6 %collective-permute-start.30 = (bf16[256,256]{1,0:T(8,128)(2,1)S(1)}, bf16[256,256]{1,0:T(8,128)(2,1)S(1)}, u32[]{:S(2)}, u32[]{:S(2)}) collective-permute-start(bf16[256,256]{1,0:T(8,128)(2,1)S(1)} %slice.34), channel_id=1, source_target_pairs={{192,0},{224,32},{0,64},{32,96},{64,128},{96,160},{128,192},{160,2... | collective-permute-start | bytes 393224 | tf_op jit(solution)/shard_map/ppermute | solution.py:48
  95.2 14.5 %collective-permute-start.31 = (bf16[256,256]{1,0:T(8,128)(2,1)S(1)}, bf16[256,256]{1,0:T(8,128)(2,1)S(1)}, u32[]{:S(2)}, u32[]{:S(2)}) collective-permute-start(bf16[256,256]{1,0:T(8,128)(2,1)S(1)} %slice.34), channel_id=1, source_target_pairs={{0,96},{32,64},{64,160},{96,128},{128,224},{160,192},{192,32},{224... | collective-permute-start | bytes 393224 | tf_op jit(solution)/shard_map/ppermute | solution.py:372
  135.7 73.7 %collective-permute-start.71 = (bf16[4,256,896]{2,1,0:T(8,128)(2,1)}, bf16[4,256,896]{2,1,0:T(8,128)(2,1)}, u32[]{:S(2)}, u32[]{:S(2)}) collective-permute-start(bf16[4,256,896]{2,1,0:T(8,128)(2,1)} %get-tuple-element.80), channel_id=1, source_target_pairs={{0,32},{32,0},{64,96},{96,64},{128,160},{160,128},{192,224},{224,1... | collective-permute-start | bytes 5505032 | tf_op jit(solution)/shard_map/ppermute | solution.py:44
  136.7 12.2 %collective-permute-start = (bf16[256,896]{1,0:T(8,128)(2,1)S(1)}, bf16[256,896]{1,0:T(8,128)(2,1)S(1)}, u32[]{:S(2)}, u32[]{:S(2)}) collective-permute-start(bf16[256,896]{1,0:T(8,128)(2,1)S(1)} %get-tuple-element.92), channel_id=1, source_target_pairs={{64,0},{96,32},{128,64},{160,96},{192,128},{224,160},{0,192},{32,2... | collective-permute-start | bytes 1376264 | tf_op jit(solution)/shard_map/ppermute | solution.py:48
  138.2 21.7 %collective-permute-start.1 = (bf16[256,896]{1,0:T(8,128)(2,1)S(1)}, bf16[256,896]{1,0:T(8,128)(2,1)S(1)}, u32[]{:S(2)}, u32[]{:S(2)}) collective-permute-start(bf16[256,896]{1,0:T(8,128)(2,1)S(1)} %get-tuple-element.91), channel_id=1, source_target_pairs={{128,0},{160,32},{192,64},{224,96},{0,128},{32,160},{64,192},{96,2... | collective-permute-start | bytes 1376264 | tf_op jit(solution)/shard_map/ppermute | solution.py:48
  139.4 21.3 %collective-permute-start.2 = (bf16[256,896]{1,0:T(8,128)(2,1)S(1)}, bf16[256,896]{1,0:T(8,128)(2,1)S(1)}, u32[]{:S(2)}, u32[]{:S(2)}) collective-permute-start(bf16[256,896]{1,0:T(8,128)(2,1)S(1)} %get-tuple-element.90), channel_id=1, source_target_pairs={{192,0},{224,32},{0,64},{32,96},{64,128},{96,160},{128,192},{160,2... | collective-permute-start | bytes 1376264 | tf_op jit(solution)/shard_map/ppermute | solution.py:48
  148.9 15.2 %collective-permute-start.4 = (bf16[256,896]{1,0:T(8,128)(2,1)S(1)}, bf16[256,896]{1,0:T(8,128)(2,1)S(1)}, u32[]{:S(2)}, u32[]{:S(2)}) collective-permute-start(bf16[256,896]{1,0:T(8,128)(2,1)S(1)} %collective-permute-done.refs_1_), channel_id=1, source_target_pairs={{0,32},{32,0},{64,96},{96,64},{128,160},{160,128},{192,224},{224,1... | collective-permute-start | bytes 1376264 | tf_op jit(solution)/shard_map/ppermute | solution.py:44
  164.1 11.9 %collective-permute-start.34 = (bf16[512,256]{1,0:T(8,128)(2,1)S(1)}, bf16[512,256]{1,0:T(8,128)(2,1)S(1)}, u32[]{:S(2)}, u32[]{:S(2)}) collective-permute-start(bf16[512,256]{1,0:T(8,128)(2,1)S(1)} %copy-done.15), channel_id=1, source_target_pairs={{128,0},{160,32},{192,64},{224,96},{0,128},{32,160},{64,192},{96,2... | collective-permute-start | bytes 786440 | tf_op jit(solution)/shard_map/ppermute | solution.py:48
  164.6 13.9 %collective-permute-start.35 = (bf16[512,256]{1,0:T(8,128)(2,1)S(1)}, bf16[512,256]{1,0:T(8,128)(2,1)S(1)}, u32[]{:S(2)}, u32[]{:S(2)}) collective-permute-start(bf16[512,256]{1,0:T(8,128)(2,1)S(1)} %copy-done.15), channel_id=1, source_target_pairs={{192,0},{224,32},{0,64},{32,96},{64,128},{96,160},{128,192},{160,2... | collective-permute-start | bytes 786440 | tf_op jit(solution)/shard_map/ppermute | solution.py:48
  166.3 14.8 %collective-permute-start.46 = (bf16[512,256]{1,0:T(8,128)(2,1)S(1)}, bf16[512,256]{1,0:T(8,128)(2,1)S(1)}, u32[]{:S(2)}, u32[]{:S(2)}) collective-permute-start(bf16[512,256]{1,0:T(8,128)(2,1)S(1)} %copy-done.3), channel_id=1, source_target_pairs={{64,0},{96,32},{128,64},{160,96},{192,128},{224,160},{0,192},{32,2... | collective-permute-start | bytes 786440 | tf_op jit(solution)/shard_map/ppermute | solution.py:48
  169.8 17.4 %collective-permute-start.47 = (bf16[512,256]{1,0:T(8,128)(2,1)S(1)}, bf16[512,256]{1,0:T(8,128)(2,1)S(1)}, u32[]{:S(2)}, u32[]{:S(2)}) collective-permute-start(bf16[512,256]{1,0:T(8,128)(2,1)S(1)} %copy-done.3), channel_id=1, source_target_pairs={{128,0},{160,32},{192,64},{224,96},{0,128},{32,160},{64,192},{96,2... | collective-permute-start | bytes 786440 | tf_op jit(solution)/shard_map/ppermute | solution.py:48
  176.0 12.8 %collective-permute-start.48 = (bf16[512,256]{1,0:T(8,128)(2,1)S(1)}, bf16[512,256]{1,0:T(8,128)(2,1)S(1)}, u32[]{:S(2)}, u32[]{:S(2)}) collective-permute-start(bf16[512,256]{1,0:T(8,128)(2,1)S(1)} %copy-done.3), channel_id=1, source_target_pairs={{192,0},{224,32},{0,64},{32,96},{64,128},{96,160},{128,192},{160,2... | collective-permute-start | bytes 786440 | tf_op jit(solution)/shard_map/ppermute | solution.py:48
  180.4 14.2 %collective-permute-start.36 = (bf16[112,256]{1,0:T(8,128)(2,1)S(1)}, bf16[112,256]{1,0:T(8,128)(2,1)S(1)}, u32[]{:S(2)}, u32[]{:S(2)}) collective-permute-start(bf16[112,256]{1,0:T(8,128)(2,1)S(1)} %get-tuple-element.52), channel_id=1, source_target_pairs={{1,0},{2,1},{3,2},{4,3},{5,4},{6,5},{7,6},{0,7},{9,8},{10,9},{11,1... | collective-permute-start | bytes 172040 | tf_op jit(solution)/shard_map/ppermute | solution.py:56
  181.1 14.8 %collective-permute-start.37 = (bf16[112,256]{1,0:T(8,128)(2,1)S(1)}, bf16[112,256]{1,0:T(8,128)(2,1)S(1)}, u32[]{:S(2)}, u32[]{:S(2)}) collective-permute-start(bf16[112,256]{1,0:T(8,128)(2,1)S(1)} %get-tuple-element.53), channel_id=1, source_target_pairs={{2,0},{3,1},{4,2},{5,3},{6,4},{7,5},{0,6},{1,7},{10,8},{11,9},{12,... | collective-permute-start | bytes 172040 | tf_op jit(solution)/shard_map/ppermute | solution.py:56
  187.2 10.7 %collective-permute-start.38 = (bf16[112,256]{1,0:T(8,128)(2,1)S(1)}, bf16[112,256]{1,0:T(8,128)(2,1)S(1)}, u32[]{:S(2)}, u32[]{:S(2)}) collective-permute-start(bf16[112,256]{1,0:T(8,128)(2,1)S(1)} %get-tuple-element.54), channel_id=1, source_target_pairs={{3,0},{4,1},{5,2},{6,3},{7,4},{0,5},{1,6},{2,7},{11,8},{12,9},{13,... | collective-permute-start | bytes 172040 | tf_op jit(solution)/shard_map/ppermute | solution.py:56
  199.0 13.6 %collective-permute-start.40 = (bf16[112,256]{1,0:T(8,128)(2,1)S(1)}, bf16[112,256]{1,0:T(8,128)(2,1)S(1)}, u32[]{:S(2)}, u32[]{:S(2)}) collective-permute-start(bf16[112,256]{1,0:T(8,128)(2,1)S(1)} %get-tuple-element.56), channel_id=1, source_target_pairs={{5,0},{6,1},{7,2},{0,3},{1,4},{2,5},{3,6},{4,7},{13,8},{14,9},{15,... | collective-permute-start | bytes 172040 | tf_op jit(solution)/shard_map/ppermute | solution.py:56
  201.7 11.0 %collective-permute-start.41 = (bf16[112,256]{1,0:T(8,128)(2,1)S(1)}, bf16[112,256]{1,0:T(8,128)(2,1)S(1)}, u32[]{:S(2)}, u32[]{:S(2)}) collective-permute-start(bf16[112,256]{1,0:T(8,128)(2,1)S(1)} %get-tuple-element.57), channel_id=1, source_target_pairs={{6,0},{7,1},{0,2},{1,3},{2,4},{3,5},{4,6},{5,7},{14,8},{15,9},{8,1... | collective-permute-start | bytes 172040 | tf_op jit(solution)/shard_map/ppermute | solution.py:56
  206.5 8.9 %collective-permute-start.60 = (f32[8,128]{1,0:T(8,128)S(1)}, f32[8,128]{1,0:T(8,128)S(1)}, u32[]{:S(2)}, u32[]{:S(2)}) collective-permute-start(f32[8,128]{1,0:T(8,128)S(1)} %add_add_fusion.1), channel_id=1, source_target_pairs={{8,0},{16,8},{24,16},{0,24},{9,1},{17,9},{25,17},{1,25},{10,2},{18... | collective-permute-start | bytes 12296 | tf_op jit(solution)/shard_map/ppermute | solution.py:52
  212.8 37.6 %collective-permute-start.49 = (bf16[112,256]{1,0:T(8,128)(2,1)S(1)}, bf16[112,256]{1,0:T(8,128)(2,1)S(1)}, u32[]{:S(2)}, u32[]{:S(2)}) collective-permute-start(bf16[112,256]{1,0:T(8,128)(2,1)S(1)} %get-tuple-element.64), channel_id=1, source_target_pairs={{1,0},{2,1},{3,2},{4,3},{5,4},{6,5},{7,6},{0,7},{9,8},{10,9},{11,1... | collective-permute-start | bytes 172040 | tf_op jit(solution)/shard_map/ppermute | solution.py:56
  215.4 71.2 %collective-permute-start.73 = (bf16[256,1024]{1,0:T(8,128)(2,1)S(1)}, bf16[256,1024]{1,0:T(8,128)(2,1)S(1)}, u32[]{:S(2)}, u32[]{:S(2)}) collective-permute-start(bf16[256,1024]{1,0:T(8,128)(2,1)S(1)} %get-tuple-element.85), channel_id=1, source_target_pairs={{8,0},{16,8},{24,16},{0,24},{9,1},{17,9},{25,17},{1,25},{10,2},{18... | collective-permute-start | bytes 1572872 | tf_op jit(solution)/shard_map/ppermute | solution.py:52
  215.7 70.9 %collective-permute-start.74 = (bf16[256,1024]{1,0:T(8,128)(2,1)S(1)}, bf16[256,1024]{1,0:T(8,128)(2,1)S(1)}, u32[]{:S(2)}, u32[]{:S(2)}) collective-permute-start(bf16[256,1024]{1,0:T(8,128)(2,1)S(1)} %get-tuple-element.86), channel_id=1, source_target_pairs={{16,0},{24,8},{0,16},{8,24},{17,1},{25,9},{1,17},{9,25},{18,2},{26... | collective-permute-start | bytes 1572872 | tf_op jit(solution)/shard_map/ppermute | solution.py:52
  217.2 69.5 %collective-permute-start.75 = (bf16[256,1024]{1,0:T(8,128)(2,1)S(1)}, bf16[256,1024]{1,0:T(8,128)(2,1)S(1)}, u32[]{:S(2)}, u32[]{:S(2)}) collective-permute-start(bf16[256,1024]{1,0:T(8,128)(2,1)S(1)} %get-tuple-element.87), channel_id=1, source_target_pairs={{24,0},{0,8},{8,16},{16,24},{25,1},{1,9},{9,17},{17,25},{26,2},{2,... | collective-permute-start | bytes 1572872 | tf_op jit(solution)/shard_map/ppermute | solution.py:52
  269.0 16.5 %collective-permute-start.70 = (f32[56,512]{1,0:T(8,128)S(1)}, f32[56,512]{1,0:T(8,128)S(1)}, u32[]{:S(2)}, u32[]{:S(2)}) collective-permute-start(f32[56,512]{1,0:T(8,128)S(1)} %get-tuple-element.74), channel_id=1, source_target_pairs={{0,32},{32,0},{64,96},{96,64},{128,160},{160,128},{192,224},{224,1... | collective-permute-start | bytes 344072 | tf_op jit(solution)/shard_map/ppermute | solution.py:44
  (75 other events, 666.1 us)

commit v2 on v1

v2 whole, which is shorter than its diff:
```python
import math

import jax
import jax.numpy as jnp
import numpy as np
from jax import lax
from jax.experimental import pallas as pl
from jax.experimental.pallas import tpu as pltpu
from jax.sharding import Mesh
from jax.sharding import PartitionSpec as P

D = 3584
H = 8
KVH = 4
HD = 256
WINDOW = 256
SLAB = D // 4
ROWS = 56
TOK = 256

EPSILON = 1e-06
SOFTCAP = 50.0
CLIP_BOUND = 1.0
ROPE_BASE = 10000.0

F32 = jnp.float32
BF16 = jnp.bfloat16
VMEM = pl.BlockSpec(memory_space=pltpu.VMEM)
SMEM = pl.BlockSpec(memory_space=pltpu.SMEM)


def call(body, outs, place, *operands, scratch=()):
    return pl.pallas_call(
        body,
        out_shape=[jax.ShapeDtypeStruct(shape, kind) for shape, kind in outs],
        in_specs=[SMEM] + [VMEM] * len(operands),
        out_specs=[VMEM] * len(outs),
        scratch_shapes=list(scratch),
        compiler_params=pltpu.CompilerParams(vmem_limit_bytes=16 * 1024 * 1024),
    )(place, *operands)


def swap(value):
    return lax.ppermute(value, "core", [(0, 1), (1, 0)])


def from_x(value, steps):
    return lax.ppermute(value, "x", [((i + steps) % 4, i) for i in range(4)])


def from_y(value, steps):
    return lax.ppermute(value, "tensor", [((i + steps) % 4, i) for i in range(4)])


def after(value, *others):
    return lax.optimization_barrier((value, *others))[0]


def code(total):
    high = total.astype(BF16)
    rest = total - high.astype(F32)
    middle = rest.astype(BF16)
    low = (rest - middle.astype(F32)).astype(BF16)
    lane = lax.broadcasted_iota(jnp.int32, total.shape, 1)
    return jnp.where(
        lane == 0,
        high.astype(F32),
        jnp.where(
            lane == 1, middle.astype(F32), jnp.where(lane == 2, low.astype(F32), jnp.zeros_like(total))
        ),
    ).astype(BF16)


def mm(a, b, contract_a=1, contract_b=0):
    return lax.dot_general(
        a, b, (((contract_a,), (contract_b,)), ((), ())), preferred_element_type=F32
    )


def norm_body(place, inputs, gain, permute, normed, moved, inverse, *apart):
    x = place[0]
    rows = inputs[...].astype(F32)
    inv = lax.rsqrt(jnp.sum(rows * rows, -1, keepdims=True) * (1.0 / D) + EPSILON)
    inverse[...] = jnp.broadcast_to(inv, inverse.shape)
    for slab in range(4):
        part = mm(inputs[:, slab * SLAB : (slab + 1) * SLAB], permute[...])
        moved[slab] = part.astype(BF16)
        normed[slab] = (part * inv * gain[slab : slab + 1, :]).astype(BF16)
    for step in range(4):
        apart[step][...] = normed[lax.rem(x + 4 - step, 4)]


def columns_body(place, *refs):
    mine, theirs, whole = refs[:4], refs[4:8], refs[8]
    x, core = place[0], place[1]
    first = pl.multiple_of(core * TOK, TOK)
    second = pl.multiple_of((1 - core) * TOK, TOK)
    for step in range(4):
        at = lax.rem(x + step, 4)
        whole[at, :, pl.ds(first, TOK)] = mine[step][...].T
        whole[at, :, pl.ds(second, TOK)] = theirs[step][...].T


def spin(value, cosine, sine, direction):
    first, second = value[:, :128], value[:, 128:]
    return jnp.concatenate(
        [first * cosine - direction * second * sine, second * cosine + direction * first * sine], -1
    )


def project_body(place, own, other, cos, sin, cos2, sin2, s0, s1, s2, s3, strip, query, pair):
    x, core = place[0], place[1]
    for rows, block in ((own, core), (other, 1 - core)):
        total_q = mm(rows[x], s0[...])
        total_p = mm(rows[0], strip[0])
        for step, slab in ((1, s1), (2, s2), (3, s3)):
            total_q += mm(rows[lax.rem(x + step, 4)], slab[...])
            total_p += mm(rows[step], strip[step])
        at = pl.ds(pl.multiple_of(block * TOK, TOK), TOK)
        query[at, :] = spin(total_q, cos[at, :], sin[at, :], 1.0).astype(BF16)
        pair[at, :] = spin(total_p, cos2[at, :], sin2[at, :], 1.0).astype(BF16)


def attend_body(place, query, mine, theirs, mine_before, theirs_before, cot, cos, sin,
                dquery, keep, keep_before, send, send_before, keys, values):
    first_core = place[1] == 0
    for at, a, b in ((0, mine_before, theirs_before), (TOK, mine, theirs)):
        rows = a.shape[0]
        keys[at : at + rows, :] = jnp.where(first_core, a[...], b[...])
        values[at : at + rows, :] = jnp.where(first_core, b[...], a[...])
    scale = 1.0 / math.sqrt(HD)
    q_at = lax.broadcasted_iota(jnp.int32, (TOK, 2 * TOK), 0)
    k_at = lax.broadcasted_iota(jnp.int32, (TOK, 2 * TOK), 1)
    band = (k_at <= q_at + TOK) & (k_at > q_at)
    key_parts = []
    value_parts = []
    for block in range(2):
        here = slice(block * TOK, (block + 1) * TOK)
        seen = slice(block * TOK, (block + 2) * TOK)
        q, g = query[here, :], cot[here, :]
        k, v = keys[seen, :], values[seen, :]
        squash = jnp.tanh(mm(q, k, 1, 1) * (scale / SOFTCAP))
        allowed = band
        if block == 0:
            allowed = band & ((k_at >= TOK) | (place[0] > 0))
        terms = jnp.where(allowed, jnp.exp(SOFTCAP * squash), 0.0)
        probs = terms / jnp.sum(terms, -1, keepdims=True)
        dprobs = mm(g, v, 1, 1)
        value_parts.append(mm(probs.astype(BF16), g, 0, 0))
        delta = jnp.sum(probs * dprobs, -1, keepdims=True)
        dlogits = (probs * (dprobs - delta) * (1.0 - squash * squash) * scale).astype(BF16)
        dq = mm(dlogits, k)
        dquery[here, :] = spin(dq, cos[here, :], sin[here, :], -1.0).astype(BF16)
        key_parts.append(mm(dlogits, q, 0, 0))

    def place_out(dk, dv, keep_at, send_at):
        keep_at[...] = jnp.where(first_core, dk, dv)
        send_at[...] = jnp.where(first_core, dv, dk).astype(BF16)

    place_out(key_parts[0][:TOK], value_parts[0][:TOK], keep_before, send_before)
    place_out(
        key_parts[0][TOK:] + key_parts[1][:TOK],
        value_parts[0][TOK:] + value_parts[1][:TOK],
        keep.at[:TOK, :],
        send.at[:TOK, :],
    )
    place_out(key_parts[1][TOK:], value_parts[1][TOK:], keep.at[TOK:, :], send.at[TOK:, :])


def halo_body(place, keep_before, got_before, out):
    out[...] = (keep_before[...] + got_before[...].astype(F32)).astype(BF16)


def pair_body(place, keep, got, back, cos2, sin2, dpair):
    for block in range(2):
        here = slice(block * TOK, (block + 1) * TOK)
        total = keep[here, :] + got[here, :].astype(F32)
        if block == 1:
            total += back[...].astype(F32)
        dpair[here, :] = spin(total, cos2[here, :], sin2[here, :], -1.0).astype(BF16)


def dnormed_body(
    place, dquery, dpair, s0, s1, s2, s3, strip, own, other, keep, send, keep_sum, send_sum
):
    x, core = place[0], place[1]
    for rows, block, out, sums in (
        (other, 1 - core, send, send_sum),
        (own, core, keep, keep_sum),
    ):
        at = pl.ds(pl.multiple_of(block * TOK, TOK), TOK)
        dq, dp = dquery[at, :], dpair[at, :]
        total = jnp.zeros((TOK, 1), F32)
        for step, slab in enumerate((s0, s1, s2, s3)):
            here = lax.rem(x + step, 4)
            part = mm(dq, slab[...], 1, 1) + mm(dp, strip[here], 1, 1)
            total += jnp.sum(part * rows[here].astype(F32), -1, keepdims=True)
            out[here] = part.astype(BF16)
        sums[...] = jnp.broadcast_to(total, sums.shape)


def split_body(place, keep, got, keep_sum, got_sum, own, own_sum, *messages):
    y = place[2]
    total = keep_sum[...] + got_sum[...]
    own_sum[...] = total
    coded = code(total)
    own[...] = keep[y].astype(F32) + got[y].astype(F32)
    for step, message in enumerate(messages):
        at = lax.rem(y + 4 - (step + 1), 4)
        message[:, :SLAB] = (keep[at].astype(F32) + got[at].astype(F32)).astype(BF16)
        message[:, SLAB:] = coded


def input_body(place, own, own_sum, m1, m2, m3, moved, inverse, gain, permute, out):
    total = own[...]
    sums = own_sum[:, :1]
    for message in (m1, m2, m3):
        total += message[:, :SLAB].astype(F32)
        sums += jnp.sum(message[:, SLAB:].astype(F32), -1, keepdims=True)
    inv = inverse[:, :1]
    y = place[2]
    rows = moved[y].astype(F32)
    grad = inv * (gain[pl.ds(y, 1), :] * total) - rows * ((inv * inv) * (sums * (1.0 / D)))
    out[0] = mm(grad.astype(BF16), permute[...], 1, 1).astype(BF16)


def weights_body(place, columns, dquery, d0, d1, d2, d3, chunks, total):
    x = place[0]
    acc = mm(columns[0], dquery[0])
    for step in range(1, 4):
        acc += mm(columns[step], dquery[step])
    square = jnp.sum(acc * acc)
    total[:, :HD] = acc
    acc = mm(columns[x], d0[...])
    for step, d in ((1, d1), (2, d2), (3, d3)):
        acc += mm(columns[lax.rem(x + step, 4)], d[...])
    square += jnp.sum(acc * acc)
    total[:, HD:] = acc
    coded = code(jnp.full((16, 2 * HD), square, F32))
    for chunk in range(8):
        chunks[chunk, :112, :] = total[chunk * 112 : (chunk + 1) * 112, :].astype(BF16)
        chunks[chunk, 112:, :] = coded


def squares_body(place, chunks, squares):
    for example in range(8):
        total = jnp.sum(chunks[example, 112:, :].astype(F32), -1, keepdims=True)
        squares[example : example + 1, :] = jnp.broadcast_to(total[:1], (1, 128))


def clip_body(place, chunks, squares, keep, send):
    core = place[1]
    rms = jnp.sqrt(squares[...] * (1.0 / (D * (H + 2 * KVH) * HD)) + EPSILON)
    factor = CLIP_BOUND / jnp.maximum(rms, CLIP_BOUND)
    total = chunks[0, :112, :].astype(F32) * factor[0:1, :1]
    for example in range(1, 8):
        total += chunks[example, :112, :].astype(F32) * factor[example : example + 1, :1]
    top, bottom = total[:ROWS], total[ROWS:]
    keep[...] = jnp.where(core == 0, top, bottom)
    send[...] = jnp.where(core == 0, bottom, top)


def out_body(place, keep, got, grad_query, grad_key, grad_value):
    first = place[1] == 0
    mine, theirs = keep[...], got[...]
    zero = jnp.where(first, mine, theirs)
    one = jnp.where(first, theirs, mine)
    grad_query[:, :HD] = zero[:, :HD]
    grad_query[:, HD:] = one[:, :HD]
    grad_key[...] = zero[:, HD:]
    grad_value[...] = one[:, HD:]


def local(inputs, w_query, w_key, w_value, norm_gain, attn_grad):
    x = lax.axis_index("x").astype(jnp.int32)
    core = lax.axis_index("core").astype(jnp.int32)
    y = lax.axis_index("tensor").astype(jnp.int32)
    z = lax.axis_index("dp").astype(jnp.int32)
    place = jnp.stack([x, core, y, z])
    first = core == 0

    low, high = w_query[:, :HD], w_query[:, HD:]
    mine = jnp.concatenate([jnp.where(first, low, high), jnp.where(first, w_key, w_value)], 1)
    theirs = jnp.concatenate([jnp.where(first, high, low), jnp.where(first, w_value, w_key)], 1)
    got = swap(theirs)
    block = jnp.concatenate([jnp.where(first, mine, got), jnp.where(first, got, mine)], 0)
    strip = lax.all_gather(block[:, HD:], ("x", "dp"), axis=0, tiled=True).reshape(4, SLAB, HD)

    index = np.arange(SLAB)
    natural = (index % 112) // ROWS * 448 + index // 112 * ROWS + index % ROWS
    permute = (
        lax.broadcasted_iota(jnp.int32, (SLAB, SLAB), 0) == jnp.asarray(natural, jnp.int32)[None, :]
    ).astype(BF16)
    gain = norm_gain.reshape(4, 2, 8, ROWS).transpose(0, 2, 1, 3).reshape(4, SLAB)
    normed, moved, inverse, *apart = call(
        norm_body,
        [((4, TOK, SLAB), BF16), ((4, TOK, SLAB), BF16), ((TOK, 128), F32)]
        + [((TOK, SLAB), BF16)] * 4,
        place,
        inputs[0],
        gain,
        permute,
    )
    columns_mine = [apart[0]] + [from_x(apart[step], step) for step in range(1, 4)]
    normed_other = swap(normed)
    columns_other = [lax.dynamic_index_in_dim(normed_other, x, 0, False)] + [
        swap(columns_mine[step]) for step in range(1, 4)
    ]
    (columns,) = call(
        columns_body, [((4, SLAB, 2 * TOK), BF16)], place, *columns_mine, *columns_other
    )

    slab = lax.all_gather(after(block[:, :HD], normed), "dp", axis=0, tiled=True)
    slabs = [slab if step == 0 else from_x(slab, step) for step in range(4)]

    cot_low, cot_high = attn_grad[0][:, :HD], attn_grad[0][:, HD:]
    cot_mine = jnp.where(first, cot_low, cot_high)
    cot_got = swap(jnp.where(first, cot_high, cot_low))
    cot = jnp.concatenate(
        [jnp.where(first, cot_mine, cot_got), jnp.where(first, cot_got, cot_mine)], 0
    )

    positions = x * (2 * TOK) + jnp.arange(2 * TOK, dtype=jnp.int32)
    frequency = ROPE_BASE ** (-2.0 * jnp.arange(HD // 2).astype(F32) / HD)
    phases = positions.astype(F32)[:, None] * frequency[None, :]
    cos, sin = jnp.cos(phases), jnp.sin(phases)
    cos2, sin2 = jnp.where(first, cos, 1.0), jnp.where(first, sin, 0.0)

    strip, columns, cot, cos, sin, cos2, sin2 = lax.optimization_barrier(
        (strip, columns, cot, cos, sin, cos2, sin2)
    )
    query, pair = call(
        project_body,
        [((2 * TOK, HD), BF16), ((2 * TOK, HD), BF16)],
        place,
        normed,
        normed_other,
        cos,
        sin,
        cos2,
        sin2,
        *slabs,
        strip,
    )
    pair_other = swap(pair)
    before = from_x(pair[TOK:], -1)
    before_other = swap(before)
    dquery, keep, keep_before, send, send_before = call(
        attend_body,
        [
            ((2 * TOK, HD), BF16),
            ((2 * TOK, HD), F32),
            ((TOK, HD), F32),
            ((2 * TOK, HD), BF16),
            ((TOK, HD), BF16),
        ],
        place,
        query,
        pair,
        pair_other,
        before,
        before_other,
        cot,
        cos,
        sin,
        scratch=[pltpu.VMEM((3 * TOK, HD), BF16), pltpu.VMEM((3 * TOK, HD), BF16)],
    )
    got_before = swap(send_before)
    got = swap(send)
    dquery_all = lax.all_gather(dquery, "x", axis=0)
    (back,) = call(halo_body, [((TOK, HD), BF16)], place, keep_before, got_before)
    back = from_x(back, 1)
    (dpair,) = call(pair_body, [((2 * TOK, HD), BF16)], place, keep, got, back, cos2, sin2)
    dpair_all = [dpair] + [from_x(dpair, step) for step in range(1, 4)]

    keep_in, send_in, keep_sum, send_sum = call(
        dnormed_body,
        [
            ((4, TOK, SLAB), BF16),
            ((4, TOK, SLAB), BF16),
            ((TOK, 128), F32),
            ((TOK, 128), F32),
        ],
        place,
        dquery,
        dpair,
        *slabs,
        strip,
        normed,
        normed_other,
    )
    got_in, got_sum = swap(send_in), swap(send_sum)
    own, own_sum, *messages = call(
        split_body,
        [((TOK, SLAB), F32), ((TOK, 128), F32)] + [((TOK, SLAB + 128), BF16)] * 3,
        place,
        keep_in,
        got_in,
        keep_sum,
        got_sum,
    )
    arrived = [from_y(message, step + 1) for step, message in enumerate(messages)]

    (chunks,) = call(
        weights_body,
        [((8, 128, 2 * HD), BF16)],
        place,
        columns,
        dquery_all,
        *dpair_all,
        scratch=[pltpu.VMEM((SLAB, 2 * HD), F32)],
    )
    chunks = after(chunks, *messages)
    chunks = lax.all_to_all(chunks, "dp", split_axis=0, concat_axis=0, tiled=True)
    (squares,) = call(squares_body, [((8, 128), F32)], place, chunks)
    for axis in ("core", "x", "tensor"):
        squares = lax.optimization_barrier(lax.psum(squares, axis))
    keep_out, send_out = call(
        clip_body,
        [((ROWS, 2 * HD), F32), ((ROWS, 2 * HD), F32)],
        place,
        chunks,
        squares,
    )
    got_out = swap(send_out)
    (input_grad,) = call(
        input_body,
        [((1, TOK, SLAB), BF16)],
        place,
        own,
        own_sum,
        *arrived,
        moved,
        inverse,
        gain,
        permute,
    )
    grad_query, grad_key, grad_value = call(
        out_body,
        [((ROWS, 2 * HD), F32), ((ROWS, HD), F32), ((ROWS, HD), F32)],
        place,
        keep_out,
        got_out,
    )
    return grad_query, grad_key, grad_value, input_grad


def solution(mesh):
    chips = Mesh(mesh.devices.reshape(4, 2, 4, 8), ("x", "core", "tensor", "dp"))
    seq = ("x", "core")
    weight = P((*seq, "dp"), "tensor")
    return jax.shard_map(
        local,
        mesh=chips,
        in_specs=(P("dp", seq, None), weight, weight, weight, P(), P("dp", seq, "tensor")),
        out_specs=(weight, weight, weight, P("dp", seq, "tensor")),
        check_vma=False,
    )
```

time: 295 us -> 263 us (0.89)
  the two profiles are of different devices: /device:TPU:11 before, /device:TPU:1 now
where the time goes in v2:
time: 263 us; the launch traced here: 262 us
  waiting for transfers between devices  85.8 us (33%)
  blocking collectives  50.2 us (19%)
  starting transfers between devices  38.9 us (15%)
  local copies, waits for them, and re-layouts  34.4 us (13%)
  Pallas kernels  30.8 us (12%)
  between operations  14.4 us (5%)
  other arithmetic  7.35 us (3%)
    ppermute x11, waiting for transfers between devices, from_x(): return lax.ppermute(value, 'x', [((i + steps) % 4, i) for i in range(4)])  36.9 us
    all_gather x1, blocking collectives, local(): lax.all_gather(after(block[:, :HD], normed), 'dp', axis=0, tiled=True)  33.6 us
    unnamed x84, local copies, waits for them, and re-layouts  33.4 us
    pallas_call x13, Pallas kernels, call(): pl.pallas_call(body, out_shape=[jax.ShapeDtypeStruct(shape, kind) for sha...  30.8 us
    all_to_all x1, waiting for transfers between devices, local(): lax.all_to_all(chunks, 'dp', split_axis=0, concat_axis=0, tiled=True)  27.7 us
    ppermute x13, starting transfers between devices, swap(): return lax.ppermute(value, 'core', [(0, 1), (1, 0)])  21.1 us
    psum x3, blocking collectives, local(): squares = lax.optimization_barrier(lax.psum(squares, axis))  16.6 us
    all_gather x1, waiting for transfers between devices, local(): lax.all_gather(block[:, HD:], ('x', 'dp'), axis=0, tiled=True)  11.8 us
  transfers between devices with their start and end apart: 30, of which 14 were waited for; matrix products, arithmetic and copies ran while one was open for 3% of the time, Pallas kernels for 6%

profile of v2, /device:TPU:1, one launch (start us, length us, event | category | flops | bytes accessed | tf_op | source)
XLA Modules:
  0.0 261.8 jit_solution(14232822406073900150)
XLA Ops:
  8.2 3.3 %collective-permute-start = (bf16[56,512]{1,0:T(8,128)(2,1)S(1)}, bf16[56,512]{1,0:T(8,128)(2,1)S(1)}, u32[]{:S(2)}, u32[]{:S(2)}) collective-permute-start(bf16[56,512]{1,0:T(8,128)(2,1)S(1)} %pad_maximum_fusion.3), channel_id=1, source_target_pairs={{0,32},{32,0},{1,33},{33,1},{2,34},{34,2},{3,35},{35,3},{4,36},{36... | collective-permute-start | bytes 172040 | tf_op jit(solution)/shard_map/ppermute | solution.py:44
  15.5 5.1 %shard_map.102 = (bf16[4,256,896]{2,1,0:T(8,128)(2,1)}, bf16[4,256,896]{2,1,0:T(8,128)(2,1)S(1)}, f32[256,128]{1,0:T(8,128)S(1)}, bf16[256,896]{1,0:T(8,128)(2,1...) custom-call(s32[4]{0:T(128)S(1)} %pad_add_fusion.place, ...), custom_call_target="tpu_custom_call" | custom-call | tf_op jit(solution)/shard_map/pallas_call | solution.py:33
  27.2 9.3 %collective-permute-done.1.refs_1_ = bf16[256,896]{1,0:T(8,128)(2,1)} collective-permute-done((bf16[256,896]{1,0:T(8,128)(2,1)}, bf16[256,896]{1,0:T(8,128)(2,1)}, u32[]{:S(2)}, u32[]{:S(2)}) %collective-permute-start.1) | collective-permute-done | bytes 458784 | tf_op jit(solution)/shard_map/ppermute | solution.py:48
  36.5 1.6 collective-permute-start.5
  38.1 1.9 broadcast_select_fusion
  40.0 33.6 %all_gather.13.s0 = bf16[896,256]{1,0:T(8,128)(2,1)} all-gather(bf16[112,256]{1,0:T(8,128)(2,1)S(1)} %get-tuple-element.51), channel_id=1, replica_groups=mesh['x'=4,'core'=2,'tensor'=4,'dp'=8] {'dp'}, dimensions={0}, use_global_device_ids=true | all-gather | bytes 516096 | tf_op jit(solution)/shard_map/all_gather | solution.py:313
  73.6 3.7 %collective-permute-start.9 = (bf16[896,256]{1,0:T(8,128)(2,1)}, bf16[896,256]{1,0:T(8,128)(2,1)}, u32[]{:S(2)}, u32[]{:S(2)}) collective-permute-start(bf16[896,256]{1,0:T(8,128)(2,1)} %all_gather.13.s0), channel_id=1, source_target_pairs={{64,0},{128,64},{192,128},{0,192},{65,1},{129,65},{193,129},{1,193... | collective-permute-start | bytes 1376264 | tf_op jit(solution)/shard_map/ppermute | solution.py:48
  77.9 6.0 %collective-permute-start.6 = (bf16[256,896]{1,0:T(8,128)(2,1)}, bf16[256,896]{1,0:T(8,128)(2,1)S(1)}, u32[]{:S(2)}, u32[]{:S(2)}) collective-permute-start(bf16[256,896]{1,0:T(8,128)(2,1)} %collective-permute-done.2.refs_2_), channel_id=1, source_target_pairs={{0,32},{32,0},{1,33},{33,1},{2,34},{34,2},{3,35},{35,3},{4,36},{36... | collective-permute-start | bytes 1376264 | tf_op jit(solution)/shard_map/ppermute | solution.py:44
  86.2 2.4 shard_map.103.columns
  88.6 1.8 copy-done
  90.4 11.8 %all-gather.4.cloned.1.call-done = bf16[3584,256]{1,0:T(8,128)(2,1)} async-done(((bf16[112,256]{1,0:T(8,128)(2,1)}), bf16[3584,256]{1,0:T(8,128)(2,1)}) %all-gather.4.cloned.1.call-update) | async-done | bytes 1835024 | tf_op jit(solution)/shard_map/all_gather | solution.py:287
  102.2 2.3 collective-permute-done.11.s3
  104.6 1.5 copy-done.2
  109.9 4.5 %shard_map.104 = (bf16[512,256]{1,0:T(8,128)(2,1)S(1)}, bf16[512,256]{1,0:T(8,128)(2,1)S(1)}) custom-call(s32[4]{0:T(128)S(1)} %pad_add_fusion.place, bf16[4,256,896]{2,1,0:T(8,128)(2,1)} %get-tuple-element.45.own, bf16[4,256,896]{2,1,0:T(8,128)(2,1)S(1)} %collective-permute-done.4.other, f32[512,128]{1,0:T(8,128)S(1)} %copy-done.11, ...), custom_call_target="tpu_custom_call" | custom-call | tf_op jit(solution)/shard_map/pallas_call | solution.py:33
  115.8 6.3 %collective-permute-done.13.mine_before = bf16[256,256]{1,0:T(8,128)(2,1)S(1)} collective-permute-done((bf16[256,256]{1,0:T(8,128)(2,1)S(1)}, bf16[256,256]{1,0:T(8,128)(2,1)S(1)}, u32[]{:S(2)}, u32[]{:S(2)}) %collective-permute-start.13) | collective-permute-done | bytes 131104 | tf_op jit(solution)/shard_map/ppermute | solution.py:48
  123.9 2.1 shard_map.105
  128.1 4.7 %collective-permute-done.17.back = bf16[256,256]{1,0:T(8,128)(2,1)S(1)} collective-permute-done((bf16[256,256]{1,0:T(8,128)(2,1)S(1)}, bf16[256,256]{1,0:T(8,128)(2,1)S(1)}, u32[]{:S(2)}, u32[]{:S(2)}) %collective-permute-start.17) | collective-permute-done | bytes 131104 | tf_op jit(solution)/shard_map/ppermute | solution.py:48
  134.2 1.5 copy-done.3
  137.6 5.6 %shard_map.109 = (bf16[4,256,896]{2,1,0:T(8,128)(2,1)S(1)}, bf16[4,256,896]{2,1,0:T(8,128)(2,1)}, f32[256,128]{1,0:T(8,128)S(1)}, f32[256,128]{1,0:T(8,128)S(1)}) custom-call(s32[4]{0:T(128)S(1)} %pad_add_fusion.place, bf16[512,256]{1,0:T(8,128)(2,1)S(1)} %copy-done.18, bf16[512,256]{1,0:T(8,128)(2,1)S(1)} %copy-done.8, bf16[896,256]{1,0:T(8,128)(2,1)} %all_gather.13.s0, ...), custom_call_target="tpu_custom_call" | custom-call | tf_op jit(solution)/shard_map/pallas_call | solution.py:33
  149.8 5.5 %collective-permute-done.18.d1 = bf16[512,256]{1,0:T(8,128)(2,1)S(1)} collective-permute-done((bf16[512,256]{1,0:T(8,128)(2,1)}, bf16[512,256]{1,0:T(8,128)(2,1)S(1)}, u32[]{:S(2)}, u32[]{:S(2)}) %collective-permute-start.18) | collective-permute-done | bytes 262176 | tf_op jit(solution)/shard_map/ppermute | solution.py:48
  155.9 1.7 collective-permute-done.19.d2
  158.4 7.0 %collective-permute-done.20.d3 = bf16[512,256]{1,0:T(8,128)(2,1)S(1)} collective-permute-done((bf16[512,256]{1,0:T(8,128)(2,1)}, bf16[512,256]{1,0:T(8,128)(2,1)S(1)}, u32[]{:S(2)}, u32[]{:S(2)}) %collective-permute-start.20) | collective-permute-done | bytes 262176 | tf_op jit(solution)/shard_map/ppermute | solution.py:48
  166.1 6.5 %all-gather.6.cloned.1.call-done = bf16[2048,256]{1,0:T(8,128)(2,1)} async-done(((bf16[512,256]{1,0:T(8,128)(2,1)}), bf16[2048,256]{1,0:T(8,128)(2,1)}) %all-gather.6.cloned.1.call-update) | async-done | bytes 1048592 | tf_op jit(solution)/shard_map/all_gather | solution.py:370
  172.6 2.0 copy-done.1
  179.7 2.7 %shard_map.108 = bf16[8,128,512]{2,1,0:T(8,128)(2,1)S(1)} custom-call(s32[4]{0:T(128)S(1)} %pad_add_fusion.place, bf16[4,896,512]{2,1,0:T(8,128)(2,1)S(1)} %copy-done.1, bf16[4,512,256]{2,1,0:T(8,128)(2,1)S(1)} %bitcast.14, bf16[512,256]{1,0:T(8,128)(2,1)S(1)} %copy-done.9, bf16[512,256]{1,0:T(8,128)(2,1)S(1)} %copy-done.26, ...), custom_call_target="tpu_custom_call" | custom-call | tf_op jit(solution)/shard_map/pallas_call | solution.py:33
  188.8 7.7 %all-to-all-start = ((bf16[8,128,512]{2,1,0:T(8,128)(2,1)}), bf16[8,128,512]{2,1,0:T(8,128)(2,1)S(1)}, u32[]{:S(2)}, u32[]{:S(2)}) async-start(bf16[8,128,512]{2,1,0:T(8,128)(2,1)} %copy-done.4), calls=%async_computation | async-start | bytes 2097152 | tf_op jit(solution)/shard_map/all_to_all | solution.py:414
  198.0 27.7 %all-to-all-done.chunks = bf16[8,128,512]{2,1,0:T(8,128)(2,1)S(1)} async-done(((bf16[8,128,512]{2,1,0:T(8,128)(2,1)}), bf16[8,128,512]{2,1,0:T(8,128)(2,1)S(1)}, u32[]{:S(2)}, u32[]{:S(2)}) %all-to-all-start) | async-done | bytes 1048608 | tf_op jit(solution)/shard_map/all_to_all | solution.py:414
  226.3 2.6 psum.21
  228.9 8.0 %psum.22 = f32[8,128]{1,0:T(8,128)S(1)} all-reduce(f32[8,128]{1,0:T(8,128)S(1)} %psum.21), channel_id=1, replica_groups=mesh['x'=4,'core'=2,'tensor'=4,'dp'=8] {'x'}, use_global_device_ids=true, to_apply=%region_1.2 | all-reduce | flops 1024 | bytes 8192 | tf_op jit(solution)/shard_map/psum | solution.py:417
  237.0 6.0 %psum.23.squares = f32[8,128]{1,0:T(8,128)S(1)} all-reduce(f32[8,128]{1,0:T(8,128)S(1)} %psum.22), channel_id=1, replica_groups=mesh['x'=4,'core'=2,'tensor'=4,'dp'=8] {'tensor'}, use_global_device_ids=true, to_apply=%region_2.3 | all-reduce | flops 1024 | bytes 8192 | tf_op jit(solution)/shard_map/psum | solution.py:417
  243.8 4.2 %collective-permute-start.23 = (f32[56,512]{1,0:T(8,128)S(1)}, f32[56,512]{1,0:T(8,128)S(1)}, u32[]{:S(2)}, u32[]{:S(2)}) collective-permute-start(f32[56,512]{1,0:T(8,128)S(1)} %get-tuple-element.70), channel_id=1, source_target_pairs={{0,32},{32,0},{1,33},{33,1},{2,34},{34,2},{3,35},{35,3},{4,36},{36... | collective-permute-start | bytes 344072 | tf_op jit(solution)/shard_map/ppermute | solution.py:44
  250.7 3.0 %shard_map.114 = bf16[1,256,896]{2,1,0:T(8,128)(2,1)} custom-call(s32[4]{0:T(128)S(1)} %pad_add_fusion.place, f32[256,896]{1,0:T(8,128)S(1)} %copy-done.22, f32[256,128]{1,0:T(8,128)S(1)} %copy-done.36, bf16[256,1024]{1,0:T(8,128)(2,1)S(1)} %collective-permute-done.24.m1, bf16[256,1024]{1,0:T(8,128)(2,1)} %collective-permute-done.25.m2, ...), custom_call_target="tpu_custom_call" | custom-call | tf_op jit(solution)/shard_map/pallas_call | solution.py:33
  (148 shorter events, 53.8 us)
Async XLA Ops:
  7.2 95.0 %all-gather.4.cloned.1.call-start = ((), (), s32[]{:S(2)}) async-start(), calls=%async_computation.1 | async-start | bytes 1892352 | tf_op jit(solution)/shard_map/all_gather | solution.py:287
  8.2 4.2 %collective-permute-start = (bf16[56,512]{1,0:T(8,128)(2,1)S(1)}, bf16[56,512]{1,0:T(8,128)(2,1)S(1)}, u32[]{:S(2)}, u32[]{:S(2)}) collective-permute-start(bf16[56,512]{1,0:T(8,128)(2,1)S(1)} %pad_maximum_fusion.3), channel_id=1, source_target_pairs={{0,32},{32,0},{1,33},{33,1},{2,34},{34,2},{3,35},{35,3},{4,36},{36... | collective-permute-start | bytes 172040 | tf_op jit(solution)/shard_map/ppermute | solution.py:44
  13.1 159.5 %all-gather.6.cloned.1.call-start = ((), (), s32[]{:S(2)}) async-start(), calls=%async_computation.2 | async-start | bytes 1310720 | tf_op jit(solution)/shard_map/all_gather | solution.py:370
  23.3 60.6 %collective-permute-start.4 = (bf16[4,256,896]{2,1,0:T(8,128)(2,1)}, bf16[4,256,896]{2,1,0:T(8,128)(2,1)S(1)}, u32[]{:S(2)}, u32[]{:S(2)}) collective-permute-start(bf16[4,256,896]{2,1,0:T(8,128)(2,1)} %get-tuple-element.45.own), channel_id=1, source_target_pairs={{0,32},{32,0},{1,33},{33,1},{2,34},{34,2},{3,35},{35,3},{4,36},{36... | collective-permute-start | bytes 5505032 | tf_op jit(solution)/shard_map/ppermute | solution.py:44
  23.6 12.9 %collective-permute-start.1 = (bf16[256,896]{1,0:T(8,128)(2,1)}, bf16[256,896]{1,0:T(8,128)(2,1)}, u32[]{:S(2)}, u32[]{:S(2)}) collective-permute-start(bf16[256,896]{1,0:T(8,128)(2,1)} %get-tuple-element.42), channel_id=1, source_target_pairs={{64,0},{128,64},{192,128},{0,192},{65,1},{129,65},{193,129},{1,193... | collective-permute-start | bytes 1376264 | tf_op jit(solution)/shard_map/ppermute | solution.py:48
  24.4 52.9 %collective-permute-start.2 = (bf16[256,896]{1,0:T(8,128)(2,1)}, bf16[256,896]{1,0:T(8,128)(2,1)}, u32[]{:S(2)}, u32[]{:S(2)}) collective-permute-start(bf16[256,896]{1,0:T(8,128)(2,1)} %get-tuple-element.43), channel_id=1, source_target_pairs={{128,0},{192,64},{0,128},{64,192},{129,1},{193,65},{1,129},{65,193... | collective-permute-start | bytes 1376264 | tf_op jit(solution)/shard_map/ppermute | solution.py:48
  24.9 52.3 %collective-permute-start.3 = (bf16[256,896]{1,0:T(8,128)(2,1)}, bf16[256,896]{1,0:T(8,128)(2,1)}, u32[]{:S(2)}, u32[]{:S(2)}) collective-permute-start(bf16[256,896]{1,0:T(8,128)(2,1)} %get-tuple-element.44), channel_id=1, source_target_pairs={{192,0},{0,64},{64,128},{128,192},{193,1},{1,65},{65,129},{129,193... | collective-permute-start | bytes 1376264 | tf_op jit(solution)/shard_map/ppermute | solution.py:48
  26.2 47.4 %collective-permute-start.8 = (bf16[256,256]{1,0:T(8,128)(2,1)}, bf16[256,256]{1,0:T(8,128)(2,1)}, u32[]{:S(2)}, u32[]{:S(2)}) collective-permute-start(bf16[256,256]{1,0:T(8,128)(2,1)} %broadcast_select_fusion.4), channel_id=1, source_target_pairs={{0,32},{32,0},{1,33},{33,1},{2,34},{34,2},{3,35},{35,3},{4,36},{36... | collective-permute-start | bytes 393224 | tf_op jit(solution)/shard_map/ppermute | solution.py:44
  36.5 41.4 %collective-permute-start.5 = (bf16[256,896]{1,0:T(8,128)(2,1)}, bf16[256,896]{1,0:T(8,128)(2,1)}, u32[]{:S(2)}, u32[]{:S(2)}) collective-permute-start(bf16[256,896]{1,0:T(8,128)(2,1)} %collective-permute-done.1.refs_1_), channel_id=1, source_target_pairs={{0,32},{32,0},{1,33},{33,1},{2,34},{34,2},{3,35},{35,3},{4,36},{36... | collective-permute-start | bytes 1376264 | tf_op jit(solution)/shard_map/ppermute | solution.py:44
  73.6 28.6 %collective-permute-start.9 = (bf16[896,256]{1,0:T(8,128)(2,1)}, bf16[896,256]{1,0:T(8,128)(2,1)}, u32[]{:S(2)}, u32[]{:S(2)}) collective-permute-start(bf16[896,256]{1,0:T(8,128)(2,1)} %all_gather.13.s0), channel_id=1, source_target_pairs={{64,0},{128,64},{192,128},{0,192},{65,1},{129,65},{193,129},{1,193... | collective-permute-start | bytes 1376264 | tf_op jit(solution)/shard_map/ppermute | solution.py:48
  77.2 25.0 %collective-permute-start.10 = (bf16[896,256]{1,0:T(8,128)(2,1)}, bf16[896,256]{1,0:T(8,128)(2,1)}, u32[]{:S(2)}, u32[]{:S(2)}) collective-permute-start(bf16[896,256]{1,0:T(8,128)(2,1)} %all_gather.13.s0), channel_id=1, source_target_pairs={{128,0},{192,64},{0,128},{64,192},{129,1},{193,65},{1,129},{65,193... | collective-permute-start | bytes 1376264 | tf_op jit(solution)/shard_map/ppermute | solution.py:48
  77.2 27.3 %collective-permute-start.11 = (bf16[896,256]{1,0:T(8,128)(2,1)}, bf16[896,256]{1,0:T(8,128)(2,1)}, u32[]{:S(2)}, u32[]{:S(2)}) collective-permute-start(bf16[896,256]{1,0:T(8,128)(2,1)} %all_gather.13.s0), channel_id=1, source_target_pairs={{192,0},{0,64},{64,128},{128,192},{193,1},{1,65},{65,129},{129,193... | collective-permute-start | bytes 1376264 | tf_op jit(solution)/shard_map/ppermute | solution.py:48
  77.9 8.1 %collective-permute-start.6 = (bf16[256,896]{1,0:T(8,128)(2,1)}, bf16[256,896]{1,0:T(8,128)(2,1)S(1)}, u32[]{:S(2)}, u32[]{:S(2)}) collective-permute-start(bf16[256,896]{1,0:T(8,128)(2,1)} %collective-permute-done.2.refs_2_), channel_id=1, source_target_pairs={{0,32},{32,0},{1,33},{33,1},{2,34},{34,2},{3,35},{35,3},{4,36},{36... | collective-permute-start | bytes 1376264 | tf_op jit(solution)/shard_map/ppermute | solution.py:44
  83.9 2.3 collective-permute-start.7
  114.4 8.5 %collective-permute-start.12 = (bf16[512,256]{1,0:T(8,128)(2,1)S(1)}, bf16[512,256]{1,0:T(8,128)(2,1)S(1)}, u32[]{:S(2)}, u32[]{:S(2)}) collective-permute-start(bf16[512,256]{1,0:T(8,128)(2,1)S(1)} %get-tuple-element.54.mine), channel_id=1, source_target_pairs={{0,32},{32,0},{1,33},{33,1},{2,34},{34,2},{3,35},{35,3},{4,36},{36... | collective-permute-start | bytes 786440 | tf_op jit(solution)/shard_map/ppermute | solution.py:44
  115.7 6.4 %collective-permute-start.13 = (bf16[256,256]{1,0:T(8,128)(2,1)S(1)}, bf16[256,256]{1,0:T(8,128)(2,1)S(1)}, u32[]{:S(2)}, u32[]{:S(2)}) collective-permute-start(bf16[256,256]{1,0:T(8,128)(2,1)S(1)} %slice.27), channel_id=1, source_target_pairs={{192,0},{0,64},{64,128},{128,192},{193,1},{1,65},{65,129},{129,193... | collective-permute-start | bytes 393224 | tf_op jit(solution)/shard_map/ppermute | solution.py:48
  122.1 1.8 collective-permute-start.14
  126.0 1.4 collective-permute-start.16
  126.5 1.7 collective-permute-start.15
  128.0 4.8 %collective-permute-start.17 = (bf16[256,256]{1,0:T(8,128)(2,1)S(1)}, bf16[256,256]{1,0:T(8,128)(2,1)S(1)}, u32[]{:S(2)}, u32[]{:S(2)}) collective-permute-start(bf16[256,256]{1,0:T(8,128)(2,1)S(1)} %shard_map.106), channel_id=1, source_target_pairs={{64,0},{128,64},{192,128},{0,192},{65,1},{129,65},{193,129},{1,193... | collective-permute-start | bytes 393224 | tf_op jit(solution)/shard_map/ppermute | solution.py:48
  145.8 37.6 %collective-permute-start.21 = (bf16[4,256,896]{2,1,0:T(8,128)(2,1)}, bf16[4,256,896]{2,1,0:T(8,128)(2,1)S(1)}, u32[]{:S(2)}, u32[]{:S(2)}) collective-permute-start(bf16[4,256,896]{2,1,0:T(8,128)(2,1)} %get-tuple-element.62), channel_id=1, source_target_pairs={{0,32},{32,0},{1,33},{33,1},{2,34},{34,2},{3,35},{35,3},{4,36},{36... | collective-permute-start | bytes 5505032 | tf_op jit(solution)/shard_map/ppermute | solution.py:44
  147.0 8.2 %collective-permute-start.18 = (bf16[512,256]{1,0:T(8,128)(2,1)}, bf16[512,256]{1,0:T(8,128)(2,1)S(1)}, u32[]{:S(2)}, u32[]{:S(2)}) collective-permute-start(bf16[512,256]{1,0:T(8,128)(2,1)} %copy-done.7), channel_id=1, source_target_pairs={{64,0},{128,64},{192,128},{0,192},{65,1},{129,65},{193,129},{1,193... | collective-permute-start | bytes 786440 | tf_op jit(solution)/shard_map/ppermute | solution.py:48
  148.3 9.4 %collective-permute-start.19 = (bf16[512,256]{1,0:T(8,128)(2,1)}, bf16[512,256]{1,0:T(8,128)(2,1)S(1)}, u32[]{:S(2)}, u32[]{:S(2)}) collective-permute-start(bf16[512,256]{1,0:T(8,128)(2,1)} %copy-done.7), channel_id=1, source_target_pairs={{128,0},{192,64},{0,128},{64,192},{129,1},{193,65},{1,129},{65,193... | collective-permute-start | bytes 786440 | tf_op jit(solution)/shard_map/ppermute | solution.py:48
  148.3 17.1 %collective-permute-start.20 = (bf16[512,256]{1,0:T(8,128)(2,1)}, bf16[512,256]{1,0:T(8,128)(2,1)S(1)}, u32[]{:S(2)}, u32[]{:S(2)}) collective-permute-start(bf16[512,256]{1,0:T(8,128)(2,1)} %copy-done.7), channel_id=1, source_target_pairs={{192,0},{0,64},{64,128},{128,192},{193,1},{1,65},{65,129},{129,193... | collective-permute-start | bytes 786440 | tf_op jit(solution)/shard_map/ppermute | solution.py:48
  149.2 34.2 %collective-permute-start.22 = (f32[256,128]{1,0:T(8,128)}, f32[256,128]{1,0:T(8,128)}, u32[]{:S(2)}, u32[]{:S(2)}) collective-permute-start(f32[256,128]{1,0:T(8,128)} %copy-done.40), channel_id=1, source_target_pairs={{0,32},{32,0},{1,33},{33,1},{2,34},{34,2},{3,35},{35,3},{4,36},{36... | collective-permute-start | bytes 393224 | tf_op jit(solution)/shard_map/ppermute | solution.py:44
  188.8 59.2 %copy-start.32 = (f32[256,128]{1,0:T(8,128)S(1)}, f32[256,128]{1,0:T(8,128)}, u32[]{:S(2)}) copy-start(f32[256,128]{1,0:T(8,128)} %copy-done.31) | copy-start | bytes 393220
  188.8 59.2 %copy-start.36 = (f32[256,128]{1,0:T(8,128)S(1)}, f32[256,128]{1,0:T(8,128)}, u32[]{:S(2)}) copy-start(f32[256,128]{1,0:T(8,128)} %copy-done.35) | copy-start | bytes 393220
  188.8 36.9 %all-to-all-start = ((bf16[8,128,512]{2,1,0:T(8,128)(2,1)}), bf16[8,128,512]{2,1,0:T(8,128)(2,1)S(1)}, u32[]{:S(2)}, u32[]{:S(2)}) async-start(bf16[8,128,512]{2,1,0:T(8,128)(2,1)} %copy-done.4), calls=%async_computation | async-start | bytes 2097152 | tf_op jit(solution)/shard_map/all_to_all | solution.py:414
  196.5 51.5 %collective-permute-start.24 = (bf16[256,1024]{1,0:T(8,128)(2,1)}, bf16[256,1024]{1,0:T(8,128)(2,1)S(1)}, u32[]{:S(2)}, u32[]{:S(2)}) collective-permute-start(bf16[256,1024]{1,0:T(8,128)(2,1)} %copy-done.39), channel_id=1, source_target_pairs={{8,0},{16,8},{24,16},{0,24},{9,1},{17,9},{25,17},{1,25},{10,2},{18... | collective-permute-start | bytes 1572872 | tf_op jit(solution)/shard_map/ppermute | solution.py:52
  196.5 51.5 %collective-permute-start.25 = (bf16[256,1024]{1,0:T(8,128)(2,1)}, bf16[256,1024]{1,0:T(8,128)(2,1)}, u32[]{:S(2)}, u32[]{:S(2)}) collective-permute-start(bf16[256,1024]{1,0:T(8,128)(2,1)} %copy-done.38), channel_id=1, source_target_pairs={{16,0},{24,8},{0,16},{8,24},{17,1},{25,9},{1,17},{9,25},{18,2},{26... | collective-permute-start | bytes 1572872 | tf_op jit(solution)/shard_map/ppermute | solution.py:52
  196.7 51.3 %collective-permute-start.26 = (bf16[256,1024]{1,0:T(8,128)(2,1)}, bf16[256,1024]{1,0:T(8,128)(2,1)}, u32[]{:S(2)}, u32[]{:S(2)}) collective-permute-start(bf16[256,1024]{1,0:T(8,128)(2,1)} %copy-done.37), channel_id=1, source_target_pairs={{24,0},{0,8},{8,16},{16,24},{25,1},{1,9},{9,17},{17,25},{26,2},{2,... | collective-permute-start | bytes 1572872 | tf_op jit(solution)/shard_map/ppermute | solution.py:52
  243.8 9.9 %collective-permute-start.23 = (f32[56,512]{1,0:T(8,128)S(1)}, f32[56,512]{1,0:T(8,128)S(1)}, u32[]{:S(2)}, u32[]{:S(2)}) collective-permute-start(f32[56,512]{1,0:T(8,128)S(1)} %get-tuple-element.70), channel_id=1, source_target_pairs={{0,32},{32,0},{1,33},{33,1},{2,34},{34,2},{3,35},{35,3},{4,36},{36... | collective-permute-start | bytes 344072 | tf_op jit(solution)/shard_map/ppermute | solution.py:44
  (40 other events, 128.9 us)
Sparse Core Ops, SparseCore 0:
  13.2 88.9 all-gather.3
  147.1 25.3 all-gather.5

commit v3 on v2

--- a/solution.py
+++ b/solution.py
@@ -25,18 +25,74 @@
 
 F32 = jnp.float32
 BF16 = jnp.bfloat16
-VMEM = pl.BlockSpec(memory_space=pltpu.VMEM)
+ANY = pl.BlockSpec(memory_space=pl.ANY)
 SMEM = pl.BlockSpec(memory_space=pltpu.SMEM)
 
 
+class Arriving:
+    def __init__(self, copy, ref):
+        self.copy, self.ref, self.here = copy, ref, False
+
+    def wait(self):
+        if not self.here:
+            self.copy.wait()
+            self.here = True
+
+    def __getitem__(self, at):
+        self.wait()
+        return self.ref[at]
+
+
+class Leaving:
+    def __init__(self, copy, ref):
+        self.copy, self.ref, self.gone = copy, ref, False
+
+    def __getitem__(self, at):
+        return self.ref[at]
+
+    def __setitem__(self, at, value):
+        self.ref[at] = value
+
+    def leave(self):
+        if not self.gone:
+            self.copy.start()
+            self.gone = True
+
+
 def call(body, outs, place, *operands, scratch=()):
+    count, made = len(operands), len(outs)
+
+    def kernel(place_ref, *refs):
+        held = refs[count + made : 2 * (count + made)]
+        sems = refs[2 * (count + made)]
+        rest = refs[2 * (count + made) + 1 :]
+        arriving = []
+        for k in range(count):
+            copy = pltpu.make_async_copy(refs[k], held[k], sems.at[k])
+            copy.start()
+            arriving.append(Arriving(copy, held[k]))
+        leaving = []
+        for k in range(count, count + made):
+            copy = pltpu.make_async_copy(held[k], refs[k], sems.at[k])
+            leaving.append(Leaving(copy, held[k]))
+        body(place_ref, *arriving, *leaving, *rest)
+        for one in leaving:
+            one.leave()
+        for one in arriving:
+            one.wait()
+        for one in leaving:
+            one.copy.wait()
+
     return pl.pallas_call(
-        body,
+        kernel,
         out_shape=[jax.ShapeDtypeStruct(shape, kind) for shape, kind in outs],
-        in_specs=[SMEM] + [VMEM] * len(operands),
-        out_specs=[VMEM] * len(outs),
-        scratch_shapes=list(scratch),
-        compiler_params=pltpu.CompilerParams(vmem_limit_bytes=16 * 1024 * 1024),
+        in_specs=[SMEM] + [ANY] * count,
+        out_specs=[ANY] * made,
+        scratch_shapes=[pltpu.VMEM(one.shape, one.dtype) for one in operands]
+        + [pltpu.VMEM(shape, kind) for shape, kind in outs]
+        + [pltpu.SemaphoreType.DMA((count + made,))]
+        + list(scratch),
+        compiler_params=pltpu.CompilerParams(vmem_limit_bytes=32 * 1024 * 1024),
     )(place, *operands)
 
 
@@ -50,6 +106,10 @@
 
 def from_y(value, steps):
     return lax.ppermute(value, "tensor", [((i + steps) % 4, i) for i in range(4)])
+
+
+def from_z(value, steps):
+    return lax.ppermute(value, "dp", [((i + steps) % 8, i) for i in range(8)])
 
 
 def after(value, *others):
@@ -77,17 +137,36 @@
     )
 
 
-def norm_body(place, inputs, gain, permute, normed, moved, inverse, *apart):
+def norm_body(place, inputs, permute, gain, normed, n0, n1, n2, n3, moved, inverse):
     x = place[0]
     rows = inputs[...].astype(F32)
     inv = lax.rsqrt(jnp.sum(rows * rows, -1, keepdims=True) * (1.0 / D) + EPSILON)
-    inverse[...] = jnp.broadcast_to(inv, inverse.shape)
+    inverse[...] = jnp.broadcast_to(inv, inverse.ref.shape)
     for slab in range(4):
         part = mm(inputs[:, slab * SLAB : (slab + 1) * SLAB], permute[...])
         moved[slab] = part.astype(BF16)
         normed[slab] = (part * inv * gain[slab : slab + 1, :]).astype(BF16)
-    for step in range(4):
-        apart[step][...] = normed[lax.rem(x + 4 - step, 4)]
+    normed.leave()
+    for step, one in enumerate((n0, n1, n2, n3)):
+        one[...] = normed[lax.rem(x + 4 - step, 4)]
+        one.leave()
+
+
+def stack_body(place, own, far, up, down, up2, down2, whole):
+    z = place[3]
+
+    def put(step, rows):
+        at = lax.rem(z + step, 8) * 112
+        whole[pl.ds(pl.multiple_of(at, 16), 112), :] = rows
+
+    put(0, own[...])
+    put(2, up2[...])
+    put(6, down2[...])
+    put(4, far[...])
+    put(1, up[:112, :])
+    put(5, up[112:, :])
+    put(7, down[:112, :])
+    put(3, down[112:, :])
 
 
 def columns_body(place, *refs):
@@ -108,24 +187,33 @@
     )
 
 
-def project_body(place, own, other, cos, sin, cos2, sin2, s0, s1, s2, s3, strip, query, pair):
+PIECES = ((0, 0, SLAB), (1, 0, SLAB), (3, 0, SLAB), (2, 0, 384), (2, 384, SLAB))
+
+
+def project_body(
+    place, own, s0, other, cos, sin, cos2, sin2, s1, s3, s2a, s2b, query, pair, total
+):
     x, core = place[0], place[1]
-    for rows, block in ((own, core), (other, 1 - core)):
-        total_q = mm(rows[x], s0[...])
-        total_p = mm(rows[0], strip[0])
-        for step, slab in ((1, s1), (2, s2), (3, s3)):
-            total_q += mm(rows[lax.rem(x + step, 4)], slab[...])
-            total_p += mm(rows[step], strip[step])
+    slabs = (s0, s1, s3, s2a, s2b)
+    for turn, ((step, start, stop), slab) in enumerate(zip(PIECES, slabs)):
+        here = lax.rem(x + step, 4)
+        for half, rows in enumerate((own, other)):
+            part = mm(rows[here, :, start:stop], slab[...])
+            total[half] = part if turn == 0 else total[half] + part
+    for half, block in ((0, core), (1, 1 - core)):
         at = pl.ds(pl.multiple_of(block * TOK, TOK), TOK)
-        query[at, :] = spin(total_q, cos[at, :], sin[at, :], 1.0).astype(BF16)
-        pair[at, :] = spin(total_p, cos2[at, :], sin2[at, :], 1.0).astype(BF16)
+        pair[at, :] = spin(total[half][:, HD:], cos2[at, :], sin2[at, :], 1.0).astype(BF16)
+    pair.leave()
+    for half, block in ((0, core), (1, 1 - core)):
+        at = pl.ds(pl.multiple_of(block * TOK, TOK), TOK)
+        query[at, :] = spin(total[half][:, :HD], cos[at, :], sin[at, :], 1.0).astype(BF16)
 
 
 def attend_body(place, query, mine, theirs, mine_before, theirs_before, cot, cos, sin,
                 dquery, keep, keep_before, send, send_before, keys, values):
     first_core = place[1] == 0
     for at, a, b in ((0, mine_before, theirs_before), (TOK, mine, theirs)):
-        rows = a.shape[0]
+        rows = a.ref.shape[0]
         keys[at : at + rows, :] = jnp.where(first_core, a[...], b[...])
         values[at : at + rows, :] = jnp.where(first_core, b[...], a[...])
     scale = 1.0 / math.sqrt(HD)
@@ -153,62 +241,66 @@
         dquery[here, :] = spin(dq, cos[here, :], sin[here, :], -1.0).astype(BF16)
         key_parts.append(mm(dlogits, q, 0, 0))
 
-    def place_out(dk, dv, keep_at, send_at):
-        keep_at[...] = jnp.where(first_core, dk, dv)
-        send_at[...] = jnp.where(first_core, dv, dk).astype(BF16)
-
-    place_out(key_parts[0][:TOK], value_parts[0][:TOK], keep_before, send_before)
+    def place_out(dk, dv, keep_at, send_at, here):
+        keep_at[here, :] = jnp.where(first_core, dk, dv)
+        send_at[here, :] = jnp.where(first_core, dv, dk).astype(BF16)
+
+    place_out(key_parts[0][:TOK], value_parts[0][:TOK], keep_before, send_before, slice(0, TOK))
     place_out(
         key_parts[0][TOK:] + key_parts[1][:TOK],
         value_parts[0][TOK:] + value_parts[1][:TOK],
-        keep.at[:TOK, :],
-        send.at[:TOK, :],
-    )
-    place_out(key_parts[1][TOK:], value_parts[1][TOK:], keep.at[TOK:, :], send.at[TOK:, :])
+        keep,
+        send,
+        slice(0, TOK),
+    )
+    place_out(key_parts[1][TOK:], value_parts[1][TOK:], keep, send, slice(TOK, 2 * TOK))
 
 
 def halo_body(place, keep_before, got_before, out):
     out[...] = (keep_before[...] + got_before[...].astype(F32)).astype(BF16)
 
 
-def pair_body(place, keep, got, back, cos2, sin2, dpair):
+def pair_body(place, dquery, keep, got, cos2, sin2, back, dout):
+    dout[:, :HD] = dquery[...]
     for block in range(2):
         here = slice(block * TOK, (block + 1) * TOK)
         total = keep[here, :] + got[here, :].astype(F32)
         if block == 1:
             total += back[...].astype(F32)
-        dpair[here, :] = spin(total, cos2[here, :], sin2[here, :], -1.0).astype(BF16)
+        dout[here, HD:] = spin(total, cos2[here, :], sin2[here, :], -1.0).astype(BF16)
 
 
 def dnormed_body(
-    place, dquery, dpair, s0, s1, s2, s3, strip, own, other, keep, send, keep_sum, send_sum
+    place, dout, s0, other, s1, s3, s2a, s2b, own, send, send_sum, keep, keep_sum
 ):
     x, core = place[0], place[1]
     for rows, block, out, sums in (
         (other, 1 - core, send, send_sum),
         (own, core, keep, keep_sum),
     ):
-        at = pl.ds(pl.multiple_of(block * TOK, TOK), TOK)
-        dq, dp = dquery[at, :], dpair[at, :]
+        d = dout[pl.ds(pl.multiple_of(block * TOK, TOK), TOK), :]
         total = jnp.zeros((TOK, 1), F32)
-        for step, slab in enumerate((s0, s1, s2, s3)):
+        for (step, start, stop), slab in zip(PIECES, (s0, s1, s3, s2a, s2b)):
             here = lax.rem(x + step, 4)
-            part = mm(dq, slab[...], 1, 1) + mm(dp, strip[here], 1, 1)
-            total += jnp.sum(part * rows[here].astype(F32), -1, keepdims=True)
-            out[here] = part.astype(BF16)
-        sums[...] = jnp.broadcast_to(total, sums.shape)
-
-
-def split_body(place, keep, got, keep_sum, got_sum, own, own_sum, *messages):
+            part = mm(d, slab[...], 1, 1)
+            total += jnp.sum(part * rows[here, :, start:stop].astype(F32), -1, keepdims=True)
+            out[here, :, start:stop] = part.astype(BF16)
+        sums[...] = jnp.broadcast_to(total, sums.ref.shape)
+        out.leave()
+        sums.leave()
+
+
+def split_body(place, keep, got, keep_sum, got_sum, m1, m2, m3, own, own_sum):
     y = place[2]
     total = keep_sum[...] + got_sum[...]
     own_sum[...] = total
     coded = code(total)
-    own[...] = keep[y].astype(F32) + got[y].astype(F32)
-    for step, message in enumerate(messages):
+    for step, message in enumerate((m1, m2, m3)):
         at = lax.rem(y + 4 - (step + 1), 4)
         message[:, :SLAB] = (keep[at].astype(F32) + got[at].astype(F32)).astype(BF16)
         message[:, SLAB:] = coded
+        message.leave()
+    own[...] = keep[y].astype(F32) + got[y].astype(F32)
 
 
 def input_body(place, own, own_sum, m1, m2, m3, moved, inverse, gain, permute, out):
@@ -224,40 +316,29 @@
     out[0] = mm(grad.astype(BF16), permute[...], 1, 1).astype(BF16)
 
 
-def weights_body(place, columns, dquery, d0, d1, d2, d3, chunks, total):
-    x = place[0]
-    acc = mm(columns[0], dquery[0])
-    for step in range(1, 4):
-        acc += mm(columns[step], dquery[step])
-    square = jnp.sum(acc * acc)
-    total[:, :HD] = acc
+def weights_body(place, d0, columns, d1, d2, d3, squares, chunks):
+    x, z = place[0], place[3]
     acc = mm(columns[x], d0[...])
     for step, d in ((1, d1), (2, d2), (3, d3)):
         acc += mm(columns[lax.rem(x + step, 4)], d[...])
-    square += jnp.sum(acc * acc)
-    total[:, HD:] = acc
-    coded = code(jnp.full((16, 2 * HD), square, F32))
     for chunk in range(8):
-        chunks[chunk, :112, :] = total[chunk * 112 : (chunk + 1) * 112, :].astype(BF16)
-        chunks[chunk, 112:, :] = coded
-
-
-def squares_body(place, chunks, squares):
-    for example in range(8):
-        total = jnp.sum(chunks[example, 112:, :].astype(F32), -1, keepdims=True)
-        squares[example : example + 1, :] = jnp.broadcast_to(total[:1], (1, 128))
-
-
-def clip_body(place, chunks, squares, keep, send):
+        chunks[chunk] = acc[chunk * 112 : (chunk + 1) * 112, :].astype(BF16)
+    chunks.leave()
+    row = lax.broadcasted_iota(jnp.int32, (8, 128), 0)
+    squares[...] = jnp.where(row == z, jnp.sum(acc * acc), 0.0)
+
+
+def clip_body(place, squares, chunks, send, keep):
     core = place[1]
     rms = jnp.sqrt(squares[...] * (1.0 / (D * (H + 2 * KVH) * HD)) + EPSILON)
     factor = CLIP_BOUND / jnp.maximum(rms, CLIP_BOUND)
-    total = chunks[0, :112, :].astype(F32) * factor[0:1, :1]
+    total = chunks[0].astype(F32) * factor[0:1, :1]
     for example in range(1, 8):
-        total += chunks[example, :112, :].astype(F32) * factor[example : example + 1, :1]
+        total += chunks[example].astype(F32) * factor[example : example + 1, :1]
     top, bottom = total[:ROWS], total[ROWS:]
+    send[...] = jnp.where(core == 0, bottom, top)
+    send.leave()
     keep[...] = jnp.where(core == 0, top, bottom)
-    send[...] = jnp.where(core == 0, bottom, top)
 
 
 def out_body(place, keep, got, grad_query, grad_key, grad_value):
@@ -284,7 +365,15 @@
     theirs = jnp.concatenate([jnp.where(first, high, low), jnp.where(first, w_value, w_key)], 1)
     got = swap(theirs)
     block = jnp.concatenate([jnp.where(first, mine, got), jnp.where(first, got, mine)], 0)
-    strip = lax.all_gather(block[:, HD:], ("x", "dp"), axis=0, tiled=True).reshape(4, SLAB, HD)
+    far = from_z(block, 4)
+    up2, down2 = from_z(block, 2), from_z(block, -2)
+    both = jnp.concatenate([block, far], 0)
+    up, down = from_z(both, 1), from_z(both, -1)
+    (slab,) = call(
+        stack_body, [((SLAB, 2 * HD), BF16)], place, block, far, up, down, up2, down2
+    )
+    right, left = from_x(slab, 1), from_x(slab, -1)
+    slabs = (slab, right, left, from_x(right[:384], 1), from_x(left[384:], -1))
 
     index = np.arange(SLAB)
     natural = (index % 112) // ROWS * 448 + index // 112 * ROWS + index % ROWS
@@ -292,14 +381,15 @@
         lax.broadcasted_iota(jnp.int32, (SLAB, SLAB), 0) == jnp.asarray(natural, jnp.int32)[None, :]
     ).astype(BF16)
     gain = norm_gain.reshape(4, 2, 8, ROWS).transpose(0, 2, 1, 3).reshape(4, SLAB)
-    normed, moved, inverse, *apart = call(
+    normed, *apart, moved, inverse = call(
         norm_body,
-        [((4, TOK, SLAB), BF16), ((4, TOK, SLAB), BF16), ((TOK, 128), F32)]
-        + [((TOK, SLAB), BF16)] * 4,
+        [((4, TOK, SLAB), BF16)]
+        + [((TOK, SLAB), BF16)] * 4
+        + [((4, TOK, SLAB), BF16), ((TOK, 128), F32)],
         place,
         inputs[0],
+        permute,
         gain,
-        permute,
     )
     columns_mine = [apart[0]] + [from_x(apart[step], step) for step in range(1, 4)]
     normed_other = swap(normed)
@@ -310,9 +400,6 @@
         columns_body, [((4, SLAB, 2 * TOK), BF16)], place, *columns_mine, *columns_other
     )
 
-    slab = lax.all_gather(after(block[:, :HD], normed), "dp", axis=0, tiled=True)
-    slabs = [slab if step == 0 else from_x(slab, step) for step in range(4)]
-
     cot_low, cot_high = attn_grad[0][:, :HD], attn_grad[0][:, HD:]
     cot_mine = jnp.where(first, cot_low, cot_high)
     cot_got = swap(jnp.where(first, cot_high, cot_low))
@@ -326,21 +413,22 @@
     cos, sin = jnp.cos(phases), jnp.sin(phases)
     cos2, sin2 = jnp.where(first, cos, 1.0), jnp.where(first, sin, 0.0)
 
-    strip, columns, cot, cos, sin, cos2, sin2 = lax.optimization_barrier(
-        (strip, columns, cot, cos, sin, cos2, sin2)
+    normed_other, columns, cot, cos, sin, cos2, sin2 = lax.optimization_barrier(
+        (normed_other, columns, cot, cos, sin, cos2, sin2)
     )
     query, pair = call(
         project_body,
         [((2 * TOK, HD), BF16), ((2 * TOK, HD), BF16)],
         place,
         normed,
+        slabs[0],
         normed_other,
         cos,
         sin,
         cos2,
         sin2,
-        *slabs,
-        strip,
+        *slabs[1:],
+        scratch=[pltpu.VMEM((2, TOK, 2 * HD), F32)],
     )
     pair_other = swap(pair)
     before = from_x(pair[TOK:], -1)
@@ -367,32 +455,27 @@
     )
     got_before = swap(send_before)
     got = swap(send)
-    dquery_all = lax.all_gather(dquery, "x", axis=0)
     (back,) = call(halo_body, [((TOK, HD), BF16)], place, keep_before, got_before)
     back = from_x(back, 1)
-    (dpair,) = call(pair_body, [((2 * TOK, HD), BF16)], place, keep, got, back, cos2, sin2)
-    dpair_all = [dpair] + [from_x(dpair, step) for step in range(1, 4)]
-
-    keep_in, send_in, keep_sum, send_sum = call(
+    (dout,) = call(
+        pair_body, [((2 * TOK, 2 * HD), BF16)], place, dquery, keep, got, cos2, sin2, back
+    )
+    dout_all = [dout] + [from_x(dout, step) for step in (1, 3, 2)]
+
+    send_in, send_sum, keep_in, keep_sum = call(
         dnormed_body,
-        [
-            ((4, TOK, SLAB), BF16),
-            ((4, TOK, SLAB), BF16),
-            ((TOK, 128), F32),
-            ((TOK, 128), F32),
-        ],
-        place,
-        dquery,
-        dpair,
-        *slabs,
-        strip,
+        [((4, TOK, SLAB), BF16), ((TOK, 128), F32)] * 2,
+        place,
+        after(dout, dout_all[1]),
+        slabs[0],
+        normed_other,
+        *slabs[1:],
         normed,
-        normed_other,
     )
     got_in, got_sum = swap(send_in), swap(send_sum)
-    own, own_sum, *messages = call(
+    *messages, own, own_sum = call(
         split_body,
-        [((TOK, SLAB), F32), ((TOK, 128), F32)] + [((TOK, SLAB + 128), BF16)] * 3,
+        [((TOK, SLAB + 128), BF16)] * 3 + [((TOK, SLAB), F32), ((TOK, 128), F32)],
         place,
         keep_in,
         got_in,
@@ -401,26 +484,25 @@
     )
     arrived = [from_y(message, step + 1) for step, message in enumerate(messages)]
 
-    (chunks,) = call(
+    squares, chunks = call(
         weights_body,
-        [((8, 128, 2 * HD), BF16)],
-        place,
+        [((8, 128), F32), ((8, 112, 2 * HD), BF16)],
+        place,
+        after(dout, *messages),
         columns,
-        dquery_all,
-        *dpair_all,
-        scratch=[pltpu.VMEM((SLAB, 2 * HD), F32)],
-    )
-    chunks = after(chunks, *messages)
+        dout_all[1],
+        dout_all[3],
+        dout_all[2],
+    )
     chunks = lax.all_to_all(chunks, "dp", split_axis=0, concat_axis=0, tiled=True)
-    (squares,) = call(squares_body, [((8, 128), F32)], place, chunks)
-    for axis in ("core", "x", "tensor"):
+    for axis in ("core", "x", "tensor", "dp"):
         squares = lax.optimization_barrier(lax.psum(squares, axis))
-    keep_out, send_out = call(
+    send_out, keep_out = call(
         clip_body,
         [((ROWS, 2 * HD), F32), ((ROWS, 2 * HD), F32)],
         place,
+        squares,
         chunks,
-        squares,
     )
     got_out = swap(send_out)
     (input_grad,) = call(

time: 263 us -> 258 us (0.981); the launches traced: 262 us -> 254 us
  starting transfers between devices: 38.9 us -> 74.2 us
  local copies, waits for them, and re-layouts: 34.4 us -> 14.6 us
  waiting for transfers between devices: 85.8 us -> 72 us
  between operations: 14.4 us -> 1.35 us
  Pallas kernels: 30.8 us -> 43.3 us
  blocking collectives: 50.2 us -> 40 us
    all_gather x1 -> x0, blocking collectives: 33.6 us -> none  [local(): lax.all_gather(after(block[:, :HD], normed), 'dp', axis=0, tiled=True)]
    all_to_all x1, waiting for transfers between devices: 27.7 us -> 0.01 us  [local(): lax.all_to_all(chunks, 'dp', split_axis=0, concat_axis=0, tiled=True)]
    unnamed x84 -> x54, local copies, waits for them, and re-layouts: 33.4 us -> 7.27 us
    ppermute x11 -> x12, waiting for transfers between devices: 36.9 us -> 60.6 us  [from_x(): return lax.ppermute(value, 'x', [((i + steps) % 4, i) for i in range(4)])]
    psum x3 -> x4, blocking collectives: 16.6 us -> 40 us  [local(): squares = lax.optimization_barrier(lax.psum(squares, axis))]
    all_gather x2 -> x0, waiting for transfers between devices: 18.3 us -> none  [the longest x1 11.8 us: local(): lax.all_gather(block[:, HD:], ('x', 'dp'), axis=0, tiled=True)]
    ppermute x13, starting transfers between devices: 21.1 us -> 36.9 us  [swap(): return lax.ppermute(value, 'core', [(0, 1), (1, 0)])]
    pallas_call x13, Pallas kernels: 30.8 us -> 43.3 us  [call(): pl.pallas_call(kernel, out_shape=[jax.ShapeDtypeStruct(shape, kind) for s...]
  transfers between devices with their start and end apart: 30 -> 34, of which waited for: 14 -> 13; matrix products, arithmetic and copies ran while one was open for 3% -> 5% of each run, Pallas kernels for 6% -> 8%
where the time goes in v3:
time: 258 us; the launch traced here: 254 us
  starting transfers between devices  74.2 us (29%)
  waiting for transfers between devices  72 us (28%)
  Pallas kernels  43.3 us (17%)
  blocking collectives  40 us (16%)
  local copies, waits for them, and re-layouts  14.6 us (6%)
  other arithmetic  8.13 us (3%)
    ppermute x12, waiting for transfers between devices, from_x(): return lax.ppermute(value, 'x', [((i + steps) % 4, i) for i in range(4)])  60.6 us
    pallas_call x13, Pallas kernels, call(): pl.pallas_call(kernel, out_shape=[jax.ShapeDtypeStruct(shape, kind) for s...  43.3 us
    psum x4, blocking collectives, local(): squares = lax.optimization_barrier(lax.psum(squares, axis))  40 us
    ppermute x13, starting transfers between devices, swap(): return lax.ppermute(value, 'core', [(0, 1), (1, 0)])  36.9 us
    ppermute x12, starting transfers between devices, from_x(): return lax.ppermute(value, 'x', [((i + steps) % 4, i) for i in range(4)])  18.4 us
    ppermute x5, starting transfers between devices, from_z(): return lax.ppermute(value, 'dp', [((i + steps) % 8, i) for i in range(8)])  9.16 us
    ppermute x5, waiting for transfers between devices, from_z(): return lax.ppermute(value, 'dp', [((i + steps) % 8, i) for i in range(8)])  8.47 us
    unnamed x54, local copies, waits for them, and re-layouts  7.27 us
  transfers between devices with their start and end apart: 34, of which 13 were waited for; matrix products, arithmetic and copies ran while one was open for 5% of the time, Pallas kernels for 8%

profile of v3, /device:TPU:1, one launch (start us, length us, event | category | flops | bytes accessed | tf_op | source)
XLA Modules:
  0.0 253.5 jit_solution(278187260053103593)
XLA Ops:
  2.2 3.2 %collective-permute-start = (bf16[56,512]{1,0:T(8,128)(2,1)}, bf16[56,512]{1,0:T(8,128)(2,1)S(1)}, u32[]{:S(2)}, u32[]{:S(2)}) collective-permute-start(bf16[56,512]{1,0:T(8,128)(2,1)} %pad_maximum_fusion.4), channel_id=1, source_target_pairs={{0,32},{32,0},{1,33},{33,1},{2,34},{34,2},{3,35},{35,3},{4,36},{36... | collective-permute-start | bytes 172040 | tf_op jit(solution)/shard_map/ppermute | solution.py:100
  7.4 5.3 %collective-permute-start.1 = (bf16[112,512]{1,0:T(8,128)(2,1)S(1)}, bf16[112,512]{1,0:T(8,128)(2,1)}, u32[]{:S(2)}, u32[]{:S(2)}) collective-permute-start(bf16[112,512]{1,0:T(8,128)(2,1)S(1)} %pad_maximum_fusion.2.refs_0_), channel_id=1, source_target_pairs={{4,0},{5,1},{6,2},{7,3},{0,4},{1,5},{2,6},{3,7},{12,8},{13,9},{14,... | collective-permute-start | bytes 344072 | tf_op jit(solution)/shard_map/ppermute | solution.py:112
  19.0 5.4 %shard_map.102 = (bf16[4,256,896]{2,1,0:T(8,128)(2,1)}, bf16[256,896]{1,0:T(8,128)(2,1)S(1)}, bf16[256,896]{1,0:T(8,128)(2,1)}, bf16[256,896]{1,0:T(8,128)(2,1)S...) custom-call(s32[4]{0:T(128)S(1)} %copy-done.15, ...), custom_call_target="tpu_custom_call" | custom-call | tf_op jit(solution)/shard_map/pallas_call | solution.py:86
  29.3 2.4 collective-permute-start.5
  31.7 8.5 %collective-permute-done.4.refs_4_ = bf16[112,512]{1,0:T(8,128)(2,1)S(1)} collective-permute-done((bf16[112,512]{1,0:T(8,128)(2,1)S(1)}, bf16[112,512]{1,0:T(8,128)(2,1)S(1)}, u32[]{:S(2)}, u32[]{:S(2)}) %collective-permute-start.4) | collective-permute-done | bytes 114720 | tf_op jit(solution)/shard_map/ppermute | solution.py:112
  40.2 2.7 %shard_map.103.refs_1_ = bf16[896,512]{1,0:T(8,128)(2,1)} custom-call(s32[4]{0:T(128)S(1)} %copy-done.15, bf16[112,512]{1,0:T(8,128)(2,1)S(1)} %pad_maximum_fusion.2.refs_0_, bf16[112,512]{1,0:T(8,128)(2,1)} %collective-permute-done.1.refs_1_, bf16[224,512]{1,0:T(8,128)(2,1)S(1)} %collective-permute-done.2.refs_2_, ...), custom_call_target="tpu_custom_call" | custom-call | tf_op jit(solution)/shard_map/pallas_call | solution.py:86
  51.1 14.2 %collective-permute-done.15.refs_8_.refs_4_ = bf16[896,512]{1,0:T(8,128)(2,1)} collective-permute-done((bf16[896,512]{1,0:T(8,128)(2,1)}, bf16[896,512]{1,0:T(8,128)(2,1)}, u32[]{:S(2)}, u32[]{:S(2)}) %collective-permute-start.15) | collective-permute-done | bytes 917536 | tf_op jit(solution)/shard_map/ppermute | solution.py:104
  71.4 3.4 %collective-permute-done.7.refs_1_ = bf16[256,896]{1,0:T(8,128)(2,1)} collective-permute-done((bf16[256,896]{1,0:T(8,128)(2,1)}, bf16[256,896]{1,0:T(8,128)(2,1)}, u32[]{:S(2)}, u32[]{:S(2)}) %collective-permute-start.7) | collective-permute-done | bytes 458784 | tf_op jit(solution)/shard_map/ppermute | solution.py:104
  74.8 11.4 %collective-permute-start.10 = (bf16[256,896]{1,0:T(8,128)(2,1)}, bf16[256,896]{1,0:T(8,128)(2,1)S(1)}, u32[]{:S(2)}, u32[]{:S(2)}) collective-permute-start(bf16[256,896]{1,0:T(8,128)(2,1)} %collective-permute-done.7.refs_1_), channel_id=1, source_target_pairs={{0,32},{32,0},{1,33},{33,1},{2,34},{34,2},{3,35},{35,3},{4,36},{36... | collective-permute-start | bytes 1376264 | tf_op jit(solution)/shard_map/ppermute | solution.py:100
  91.4 3.7 %shard_map.104.refs_1_ = bf16[4,896,512]{2,1,0:T(8,128)(2,1)S(1)} custom-call(s32[4]{0:T(128)S(1)} %copy-done.16, bf16[256,896]{1,0:T(8,128)(2,1)S(1)} %copy-done.8, bf16[256,896]{1,0:T(8,128)(2,1)} %collective-permute-done.7.refs_1_, bf16[256,896]{1,0:T(8,128)(2,1)} %collective-permute-done.8.refs_2_, bf16[256,896]{1,0:T(8,128)(2,1)} %collective-permute-done.9.refs_3_, ...), custom_call_target="tpu_custom_call" | custom-call | tf_op jit(solution)/shard_map/pallas_call | solution.py:86
  95.0 3.7 %collective-permute-done.16.refs_9_.refs_5_ = bf16[384,512]{1,0:T(8,128)(2,1)S(1)} collective-permute-done((bf16[384,512]{1,0:T(8,128)(2,1)S(1)}, bf16[384,512]{1,0:T(8,128)(2,1)S(1)}, u32[]{:S(2)}, u32[]{:S(2)}) %collective-permute-start.16) | collective-permute-done | bytes 393248 | tf_op jit(solution)/shard_map/ppermute | solution.py:104
  98.8 5.3 %shard_map.105 = (bf16[512,256]{1,0:T(8,128)(2,1)S(1)}, bf16[512,256]{1,0:T(8,128)(2,1)S(1)}) custom-call(s32[4]{0:T(128)S(1)} %copy-done.16, bf16[4,256,896]{2,1,0:T(8,128)(2,1)} %get-tuple-element.43.refs_0_.refs_7_, bf16[896,512]{1,0:T(8,128)(2,1)} %shard_map.103.refs_1_, bf16[4,256,896]{2,1,0:T(8,128)(2,1)S(1)} %collective-permute-done.6.refs_2_, ...), custom_call_target="tpu_custom_call" | custom-call | tf_op jit(solution)/shard_map/pallas_call | solution.py:86
  105.8 6.2 %collective-permute-done.19.refs_3_ = bf16[256,256]{1,0:T(8,128)(2,1)S(1)} collective-permute-done((bf16[256,256]{1,0:T(8,128)(2,1)S(1)}, bf16[256,256]{1,0:T(8,128)(2,1)S(1)}, u32[]{:S(2)}, u32[]{:S(2)}) %collective-permute-start.19) | collective-permute-done | bytes 131104 | tf_op jit(solution)/shard_map/ppermute | solution.py:104
  113.7 3.3 %shard_map.106 = (bf16[512,256]{1,0:T(8,128)(2,1)S(1)}, f32[512,256]{1,0:T(8,128)S(1)}, f32[256,256]{1,0:T(8,128)S(1)}, bf16[512,256]{1,0:T(8,128)(2,1)S(1)}, bf16[256,256]{1,0:T(8,128)(2,1)S(1)}) custom-call(s32[4]{0:T(128)S(1)} %copy-done.16, bf16[512,256]{1,0:T(8,128)(2,1)S(1)} %get-tuple-element.53.refs_0_, ...), custom_call_target="tpu_custom_call" | custom-call | tf_op jit(solution)/shard_map/pallas_call | solution.py:86
  117.0 9.4 %collective-permute-start.22 = (bf16[256,256]{1,0:T(8,128)(2,1)S(1)}, bf16[256,256]{1,0:T(8,128)(2,1)S(1)}, u32[]{:S(2)}, u32[]{:S(2)}) collective-permute-start(bf16[256,256]{1,0:T(8,128)(2,1)S(1)} %get-tuple-element.60), channel_id=1, source_target_pairs={{0,32},{32,0},{1,33},{33,1},{2,34},{34,2},{3,35},{35,3},{4,36},{36... | collective-permute-start | bytes 393224 | tf_op jit(solution)/shard_map/ppermute | solution.py:100
  129.9 3.2 %collective-permute-done.23.refs_5_ = bf16[256,256]{1,0:T(8,128)(2,1)S(1)} collective-permute-done((bf16[256,256]{1,0:T(8,128)(2,1)S(1)}, bf16[256,256]{1,0:T(8,128)(2,1)S(1)}, u32[]{:S(2)}, u32[]{:S(2)}) %collective-permute-start.23) | collective-permute-done | bytes 131104 | tf_op jit(solution)/shard_map/ppermute | solution.py:104
  134.3 2.8 %collective-permute-start.24 = (bf16[512,512]{1,0:T(8,128)(2,1)S(1)}, bf16[512,512]{1,0:T(8,128)(2,1)S(1)}, u32[]{:S(2)}, u32[]{:S(2)}) collective-permute-start(bf16[512,512]{1,0:T(8,128)(2,1)S(1)} %shard_map.108.refs_0_), channel_id=1, source_target_pairs={{64,0},{128,64},{192,128},{0,192},{65,1},{129,65},{193,129},{1,193... | collective-permute-start | bytes 1572872 | tf_op jit(solution)/shard_map/ppermute | solution.py:104
  137.0 10.0 %collective-permute-done.24.refs_2_ = bf16[512,512]{1,0:T(8,128)(2,1)S(1)} collective-permute-done((bf16[512,512]{1,0:T(8,128)(2,1)S(1)}, bf16[512,512]{1,0:T(8,128)(2,1)S(1)}, u32[]{:S(2)}, u32[]{:S(2)}) %collective-permute-start.24) | collective-permute-done | bytes 524320 | tf_op jit(solution)/shard_map/ppermute | solution.py:104
  147.1 6.7 %shard_map.109 = (bf16[4,256,896]{2,1,0:T(8,128)(2,1)S(1)}, f32[256,128]{1,0:T(8,128)S(1)}, bf16[4,256,896]{2,1,0:T(8,128)(2,1)S(1)}, f32[256,128]{1,0:T(8,128)S(1)}) custom-call(s32[4]{0:T(128)S(1)} %copy-done.16, bf16[512,512]{1,0:T(8,128)(2,1)S(1)} %shard_map.108.refs_0_, bf16[896,512]{1,0:T(8,128)(2,1)} %shard_map.103.refs_1_, ...), custom_call_target="tpu_custom_call" | custom-call | tf_op jit(solution)/shard_map/pallas_call | solution.py:86
  153.7 2.2 collective-permute-start.25
  161.6 2.3 shard_map.110
  163.9 7.1 %collective-permute-done.27.refs_3_ = bf16[512,512]{1,0:T(8,128)(2,1)S(1)} collective-permute-done((bf16[512,512]{1,0:T(8,128)(2,1)S(1)}, bf16[512,512]{1,0:T(8,128)(2,1)S(1)}, u32[]{:S(2)}, u32[]{:S(2)}) %collective-permute-start.27) | collective-permute-done | bytes 524320 | tf_op jit(solution)/shard_map/ppermute | solution.py:104
  171.0 11.6 %collective-permute-done.28.refs_4_ = bf16[512,512]{1,0:T(8,128)(2,1)S(1)} collective-permute-done((bf16[512,512]{1,0:T(8,128)(2,1)S(1)}, bf16[512,512]{1,0:T(8,128)(2,1)S(1)}, u32[]{:S(2)}, u32[]{:S(2)}) %collective-permute-start.28) | collective-permute-done | bytes 524320 | tf_op jit(solution)/shard_map/ppermute | solution.py:104
  182.6 4.3 %shard_map.111 = (f32[8,128]{1,0:T(8,128)S(1)}, bf16[8,112,512]{2,1,0:T(8,128)(2,1)}) custom-call(s32[4]{0:T(128)S(1)} %copy-done.16, bf16[512,512]{1,0:T(8,128)(2,1)S(1)} %shard_map.108.refs_0_, bf16[4,896,512]{2,1,0:T(8,128)(2,1)S(1)} %shard_map.104.refs_1_, bf16[512,512]{1,0:T(8,128)(2,1)S(1)} %collective-permute-done.24.refs_2_, ...), custom_call_target="tpu_custom_call" | custom-call | tf_op jit(solution)/shard_map/pallas_call | solution.py:86
  186.9 5.8 %all-to-all-start = ((bf16[8,112,512]{2,1,0:T(8,128)(2,1)}), bf16[8,112,512]{2,1,0:T(8,128)(2,1)S(1)}, u32[]{:S(2)}, u32[]{:S(2)}) async-start(bf16[8,112,512]{2,1,0:T(8,128)(2,1)} %get-tuple-element.72), calls=%async_computation | async-start | bytes 1835008 | tf_op jit(solution)/shard_map/all_to_all | solution.py:497
  192.8 2.7 %collective-permute-start.30 = (bf16[256,1024]{1,0:T(8,128)(2,1)}, bf16[256,1024]{1,0:T(8,128)(2,1)}, u32[]{:S(2)}, u32[]{:S(2)}) collective-permute-start(bf16[256,1024]{1,0:T(8,128)(2,1)} %copy-done.19), channel_id=1, source_target_pairs={{8,0},{16,8},{24,16},{0,24},{9,1},{17,9},{25,17},{1,25},{10,2},{18... | collective-permute-start | bytes 1572872 | tf_op jit(solution)/shard_map/ppermute | solution.py:108
  196.7 3.7 %psum.28 = f32[8,128]{1,0:T(8,128)S(1)} all-reduce(f32[8,128]{1,0:T(8,128)S(1)} %get-tuple-element.71), channel_id=1, replica_groups=mesh['x'=4,'core'=2,'tensor'=4,'dp'=8] {'core'}, use_global_device_ids=true, to_apply=%region_0.1 | all-reduce | flops 1024 | bytes 8192 | tf_op jit(solution)/shard_map/psum | solution.py:499
  200.4 7.2 %psum.29 = f32[8,128]{1,0:T(8,128)S(1)} all-reduce(f32[8,128]{1,0:T(8,128)S(1)} %psum.28), channel_id=1, replica_groups=mesh['x'=4,'core'=2,'tensor'=4,'dp'=8] {'x'}, use_global_device_ids=true, to_apply=%region_1.2 | all-reduce | flops 1024 | bytes 8192 | tf_op jit(solution)/shard_map/psum | solution.py:499
  207.6 15.6 %psum.30 = f32[8,128]{1,0:T(8,128)S(1)} all-reduce(f32[8,128]{1,0:T(8,128)S(1)} %psum.29), channel_id=1, replica_groups=mesh['x'=4,'core'=2,'tensor'=4,'dp'=8] {'tensor'}, use_global_device_ids=true, to_apply=%region_2.3 | all-reduce | flops 1024 | bytes 8192 | tf_op jit(solution)/shard_map/psum | solution.py:499
  223.3 13.5 %psum.31.refs_0_ = f32[8,128]{1,0:T(8,128)S(1)} all-reduce(f32[8,128]{1,0:T(8,128)S(1)} %psum.30), channel_id=1, replica_groups=mesh['x'=4,'core'=2,'tensor'=4,'dp'=8] {'dp'}, use_global_device_ids=true, to_apply=%region_3.4 | all-reduce | flops 1024 | bytes 8192 | tf_op jit(solution)/shard_map/psum | solution.py:499
  238.2 5.6 %collective-permute-start.29 = (f32[56,512]{1,0:T(8,128)S(1)}, f32[56,512]{1,0:T(8,128)S(1)}, u32[]{:S(2)}, u32[]{:S(2)}) collective-permute-start(f32[56,512]{1,0:T(8,128)S(1)} %get-tuple-element.74), channel_id=1, source_target_pairs={{0,32},{32,0},{1,33},{33,1},{2,34},{34,2},{3,35},{35,3},{4,36},{36... | collective-permute-start | bytes 344072 | tf_op jit(solution)/shard_map/ppermute | solution.py:100
  247.1 4.6 %shard_map.114 = bf16[1,256,896]{2,1,0:T(8,128)(2,1)} custom-call(s32[4]{0:T(128)S(1)} %copy-done.16, f32[256,896]{1,0:T(8,128)S(1)} %get-tuple-element.78.refs_0_, f32[256,128]{1,0:T(8,128)S(1)} %copy-done.12, bf16[256,1024]{1,0:T(8,128)(2,1)} %collective-permute-done.30.refs_2_, bf16[256,1024]{1,0:T(8,128)(2,1)} %collective-permute-done.31.refs_3_, ...), custom_call_target="tpu_custom_call" | custom-call | tf_op jit(solution)/shard_map/pallas_call | solution.py:86
  (127 shorter events, 55.4 us)
Async XLA Ops:
  2.2 4.5 %collective-permute-start = (bf16[56,512]{1,0:T(8,128)(2,1)}, bf16[56,512]{1,0:T(8,128)(2,1)S(1)}, u32[]{:S(2)}, u32[]{:S(2)}) collective-permute-start(bf16[56,512]{1,0:T(8,128)(2,1)} %pad_maximum_fusion.4), channel_id=1, source_target_pairs={{0,32},{32,0},{1,33},{33,1},{2,34},{34,2},{3,35},{35,3},{4,36},{36... | collective-permute-start | bytes 172040 | tf_op jit(solution)/shard_map/ppermute | solution.py:100
  7.4 19.4 %collective-permute-start.1 = (bf16[112,512]{1,0:T(8,128)(2,1)S(1)}, bf16[112,512]{1,0:T(8,128)(2,1)}, u32[]{:S(2)}, u32[]{:S(2)}) collective-permute-start(bf16[112,512]{1,0:T(8,128)(2,1)S(1)} %pad_maximum_fusion.2.refs_0_), channel_id=1, source_target_pairs={{4,0},{5,1},{6,2},{7,3},{0,4},{1,5},{2,6},{3,7},{12,8},{13,9},{14,... | collective-permute-start | bytes 344072 | tf_op jit(solution)/shard_map/ppermute | solution.py:112
  26.3 61.7 %collective-permute-start.6 = (bf16[4,256,896]{2,1,0:T(8,128)(2,1)}, bf16[4,256,896]{2,1,0:T(8,128)(2,1)S(1)}, u32[]{:S(2)}, u32[]{:S(2)}) collective-permute-start(bf16[4,256,896]{2,1,0:T(8,128)(2,1)} %get-tuple-element.43.refs_0_.refs_7_), channel_id=1, source_target_pairs={{0,32},{32,0},{1,33},{33,1},{2,34},{34,2},{3,35},{35,3},{4,36},{36... | collective-permute-start | bytes 5505032 | tf_op jit(solution)/shard_map/ppermute | solution.py:100
  27.8 12.4 %collective-permute-start.2 = (bf16[224,512]{1,0:T(8,128)(2,1)S(1)}, bf16[224,512]{1,0:T(8,128)(2,1)S(1)}, u32[]{:S(2)}, u32[]{:S(2)}) collective-permute-start(bf16[224,512]{1,0:T(8,128)(2,1)S(1)} %pad_maximum_fusion.1), channel_id=1, source_target_pairs={{1,0},{2,1},{3,2},{4,3},{5,4},{6,5},{7,6},{0,7},{9,8},{10,9},{11,1... | collective-permute-start | bytes 688136 | tf_op jit(solution)/shard_map/ppermute | solution.py:112
  27.9 12.3 %collective-permute-start.3 = (bf16[224,512]{1,0:T(8,128)(2,1)S(1)}, bf16[224,512]{1,0:T(8,128)(2,1)S(1)}, u32[]{:S(2)}, u32[]{:S(2)}) collective-permute-start(bf16[224,512]{1,0:T(8,128)(2,1)S(1)} %pad_maximum_fusion.1), channel_id=1, source_target_pairs={{7,0},{0,1},{1,2},{2,3},{3,4},{4,5},{5,6},{6,7},{15,8},{8,9},{9,10... | collective-permute-start | bytes 688136 | tf_op jit(solution)/shard_map/ppermute | solution.py:112
  29.3 10.8 %collective-permute-start.4 = (bf16[112,512]{1,0:T(8,128)(2,1)S(1)}, bf16[112,512]{1,0:T(8,128)(2,1)S(1)}, u32[]{:S(2)}, u32[]{:S(2)}) collective-permute-start(bf16[112,512]{1,0:T(8,128)(2,1)S(1)} %pad_maximum_fusion.2.refs_0_), channel_id=1, source_target_pairs={{2,0},{3,1},{4,2},{5,3},{6,4},{7,5},{0,6},{1,7},{10,8},{11,9},{12,... | collective-permute-start | bytes 344072 | tf_op jit(solution)/shard_map/ppermute | solution.py:112
  29.3 10.8 %collective-permute-start.5 = (bf16[112,512]{1,0:T(8,128)(2,1)S(1)}, bf16[112,512]{1,0:T(8,128)(2,1)S(1)}, u32[]{:S(2)}, u32[]{:S(2)}) collective-permute-start(bf16[112,512]{1,0:T(8,128)(2,1)S(1)} %pad_maximum_fusion.2.refs_0_), channel_id=1, source_target_pairs={{6,0},{7,1},{0,2},{1,3},{2,4},{3,5},{4,6},{5,7},{14,8},{15,9},{8,1... | collective-permute-start | bytes 344072 | tf_op jit(solution)/shard_map/ppermute | solution.py:112
  42.9 22.4 %collective-permute-start.15 = (bf16[896,512]{1,0:T(8,128)(2,1)}, bf16[896,512]{1,0:T(8,128)(2,1)}, u32[]{:S(2)}, u32[]{:S(2)}) collective-permute-start(bf16[896,512]{1,0:T(8,128)(2,1)} %shard_map.103.refs_1_), channel_id=1, source_target_pairs={{192,0},{0,64},{64,128},{128,192},{193,1},{1,65},{65,129},{129,193... | collective-permute-start | bytes 2752520 | tf_op jit(solution)/shard_map/ppermute | solution.py:104
  44.2 23.0 %collective-permute-start.14 = (bf16[896,512]{1,0:T(8,128)(2,1)}, bf16[896,512]{1,0:T(8,128)(2,1)}, u32[]{:S(2)}, u32[]{:S(2)}) collective-permute-start(bf16[896,512]{1,0:T(8,128)(2,1)} %shard_map.103.refs_1_), channel_id=1, source_target_pairs={{64,0},{128,64},{192,128},{0,192},{65,1},{129,65},{193,129},{1,193... | collective-permute-start | bytes 2752520 | tf_op jit(solution)/shard_map/ppermute | solution.py:104
  46.3 3.0 %collective-permute-start.13 = (bf16[256,256]{1,0:T(8,128)(2,1)}, bf16[256,256]{1,0:T(8,128)(2,1)}, u32[]{:S(2)}, u32[]{:S(2)}) collective-permute-start(bf16[256,256]{1,0:T(8,128)(2,1)} %broadcast_select_fusion.4), channel_id=1, source_target_pairs={{0,32},{32,0},{1,33},{33,1},{2,34},{34,2},{3,35},{35,3},{4,36},{36... | collective-permute-start | bytes 393224 | tf_op jit(solution)/shard_map/ppermute | solution.py:100
  48.0 26.8 %collective-permute-start.7 = (bf16[256,896]{1,0:T(8,128)(2,1)}, bf16[256,896]{1,0:T(8,128)(2,1)}, u32[]{:S(2)}, u32[]{:S(2)}) collective-permute-start(bf16[256,896]{1,0:T(8,128)(2,1)} %get-tuple-element.45), channel_id=1, source_target_pairs={{64,0},{128,64},{192,128},{0,192},{65,1},{129,65},{193,129},{1,193... | collective-permute-start | bytes 1376264 | tf_op jit(solution)/shard_map/ppermute | solution.py:104
  49.3 36.9 %collective-permute-start.8 = (bf16[256,896]{1,0:T(8,128)(2,1)}, bf16[256,896]{1,0:T(8,128)(2,1)}, u32[]{:S(2)}, u32[]{:S(2)}) collective-permute-start(bf16[256,896]{1,0:T(8,128)(2,1)} %copy-done.21), channel_id=1, source_target_pairs={{128,0},{192,64},{0,128},{64,192},{129,1},{193,65},{1,129},{65,193... | collective-permute-start | bytes 1376264 | tf_op jit(solution)/shard_map/ppermute | solution.py:104
  65.2 22.2 %collective-permute-start.9 = (bf16[256,896]{1,0:T(8,128)(2,1)}, bf16[256,896]{1,0:T(8,128)(2,1)}, u32[]{:S(2)}, u32[]{:S(2)}) collective-permute-start(bf16[256,896]{1,0:T(8,128)(2,1)} %copy-done.20), channel_id=1, source_target_pairs={{192,0},{0,64},{64,128},{128,192},{193,1},{1,65},{65,129},{129,193... | collective-permute-start | bytes 1376264 | tf_op jit(solution)/shard_map/ppermute | solution.py:104
  67.2 31.6 %collective-permute-start.17 = (bf16[512,512]{1,0:T(8,128)(2,1)}, bf16[512,512]{1,0:T(8,128)(2,1)}, u32[]{:S(2)}, u32[]{:S(2)}) collective-permute-start(bf16[512,512]{1,0:T(8,128)(2,1)} %slice.31), channel_id=1, source_target_pairs={{192,0},{0,64},{64,128},{128,192},{193,1},{1,65},{65,129},{129,193... | collective-permute-start | bytes 1572872 | tf_op jit(solution)/shard_map/ppermute | solution.py:104
  74.8 16.5 %collective-permute-start.10 = (bf16[256,896]{1,0:T(8,128)(2,1)}, bf16[256,896]{1,0:T(8,128)(2,1)S(1)}, u32[]{:S(2)}, u32[]{:S(2)}) collective-permute-start(bf16[256,896]{1,0:T(8,128)(2,1)} %collective-permute-done.7.refs_1_), channel_id=1, source_target_pairs={{0,32},{32,0},{1,33},{33,1},{2,34},{34,2},{3,35},{35,3},{4,36},{36... | collective-permute-start | bytes 1376264 | tf_op jit(solution)/shard_map/ppermute | solution.py:100
  86.2 5.1 %collective-permute-start.11 = (bf16[256,896]{1,0:T(8,128)(2,1)}, bf16[256,896]{1,0:T(8,128)(2,1)S(1)}, u32[]{:S(2)}, u32[]{:S(2)}) collective-permute-start(bf16[256,896]{1,0:T(8,128)(2,1)} %collective-permute-done.8.refs_2_), channel_id=1, source_target_pairs={{0,32},{32,0},{1,33},{33,1},{2,34},{34,2},{3,35},{35,3},{4,36},{36... | collective-permute-start | bytes 1376264 | tf_op jit(solution)/shard_map/ppermute | solution.py:100
  87.4 3.9 %collective-permute-start.12 = (bf16[256,896]{1,0:T(8,128)(2,1)}, bf16[256,896]{1,0:T(8,128)(2,1)S(1)}, u32[]{:S(2)}, u32[]{:S(2)}) collective-permute-start(bf16[256,896]{1,0:T(8,128)(2,1)} %collective-permute-done.9.refs_3_), channel_id=1, source_target_pairs={{0,32},{32,0},{1,33},{33,1},{2,34},{34,2},{3,35},{35,3},{4,36},{36... | collective-permute-start | bytes 1376264 | tf_op jit(solution)/shard_map/ppermute | solution.py:100
  88.0 10.7 %collective-permute-start.16 = (bf16[384,512]{1,0:T(8,128)(2,1)S(1)}, bf16[384,512]{1,0:T(8,128)(2,1)S(1)}, u32[]{:S(2)}, u32[]{:S(2)}) collective-permute-start(bf16[384,512]{1,0:T(8,128)(2,1)S(1)} %slice.30), channel_id=1, source_target_pairs={{64,0},{128,64},{192,128},{0,192},{65,1},{129,65},{193,129},{1,193... | collective-permute-start | bytes 1179656 | tf_op jit(solution)/shard_map/ppermute | solution.py:104
  104.1 8.7 %collective-permute-start.18 = (bf16[512,256]{1,0:T(8,128)(2,1)S(1)}, bf16[512,256]{1,0:T(8,128)(2,1)S(1)}, u32[]{:S(2)}, u32[]{:S(2)}) collective-permute-start(bf16[512,256]{1,0:T(8,128)(2,1)S(1)} %get-tuple-element.54.refs_1_), channel_id=1, source_target_pairs={{0,32},{32,0},{1,33},{33,1},{2,34},{34,2},{3,35},{35,3},{4,36},{36... | collective-permute-start | bytes 786440 | tf_op jit(solution)/shard_map/ppermute | solution.py:100
  105.0 7.1 %collective-permute-start.19 = (bf16[256,256]{1,0:T(8,128)(2,1)S(1)}, bf16[256,256]{1,0:T(8,128)(2,1)S(1)}, u32[]{:S(2)}, u32[]{:S(2)}) collective-permute-start(bf16[256,256]{1,0:T(8,128)(2,1)S(1)} %slice.27), channel_id=1, source_target_pairs={{192,0},{0,64},{64,128},{128,192},{193,1},{1,65},{65,129},{129,193... | collective-permute-start | bytes 393224 | tf_op jit(solution)/shard_map/ppermute | solution.py:104
  117.0 10.4 %collective-permute-start.22 = (bf16[256,256]{1,0:T(8,128)(2,1)S(1)}, bf16[256,256]{1,0:T(8,128)(2,1)S(1)}, u32[]{:S(2)}, u32[]{:S(2)}) collective-permute-start(bf16[256,256]{1,0:T(8,128)(2,1)S(1)} %get-tuple-element.60), channel_id=1, source_target_pairs={{0,32},{32,0},{1,33},{33,1},{2,34},{34,2},{3,35},{35,3},{4,36},{36... | collective-permute-start | bytes 393224 | tf_op jit(solution)/shard_map/ppermute | solution.py:100
  126.4 3.5 %collective-permute-start.21 = (bf16[512,256]{1,0:T(8,128)(2,1)S(1)}, bf16[512,256]{1,0:T(8,128)(2,1)S(1)}, u32[]{:S(2)}, u32[]{:S(2)}) collective-permute-start(bf16[512,256]{1,0:T(8,128)(2,1)S(1)} %get-tuple-element.58), channel_id=1, source_target_pairs={{0,32},{32,0},{1,33},{33,1},{2,34},{34,2},{3,35},{35,3},{4,36},{36... | collective-permute-start | bytes 786440 | tf_op jit(solution)/shard_map/ppermute | solution.py:100
  128.3 4.8 %collective-permute-start.23 = (bf16[256,256]{1,0:T(8,128)(2,1)S(1)}, bf16[256,256]{1,0:T(8,128)(2,1)S(1)}, u32[]{:S(2)}, u32[]{:S(2)}) collective-permute-start(bf16[256,256]{1,0:T(8,128)(2,1)S(1)} %shard_map.107), channel_id=1, source_target_pairs={{64,0},{128,64},{192,128},{0,192},{65,1},{129,65},{193,129},{1,193... | collective-permute-start | bytes 393224 | tf_op jit(solution)/shard_map/ppermute | solution.py:104
  134.3 12.8 %collective-permute-start.24 = (bf16[512,512]{1,0:T(8,128)(2,1)S(1)}, bf16[512,512]{1,0:T(8,128)(2,1)S(1)}, u32[]{:S(2)}, u32[]{:S(2)}) collective-permute-start(bf16[512,512]{1,0:T(8,128)(2,1)S(1)} %shard_map.108.refs_0_), channel_id=1, source_target_pairs={{64,0},{128,64},{192,128},{0,192},{65,1},{129,65},{193,129},{1,193... | collective-permute-start | bytes 1572872 | tf_op jit(solution)/shard_map/ppermute | solution.py:104
  153.7 7.8 %collective-permute-start.25 = (bf16[4,256,896]{2,1,0:T(8,128)(2,1)S(1)}, bf16[4,256,896]{2,1,0:T(8,128)(2,1)S(1)}, u32[]{:S(2)}, u32[]{:S(2)}) collective-permute-start(bf16[4,256,896]{2,1,0:T(8,128)(2,1)S(1)} %get-tuple-element.63), channel_id=1, source_target_pairs={{0,32},{32,0},{1,33},{33,1},{2,34},{34,2},{3,35},{35,3},{4,36},{36... | collective-permute-start | bytes 5505032 | tf_op jit(solution)/shard_map/ppermute | solution.py:100
  155.9 15.0 %collective-permute-start.27 = (bf16[512,512]{1,0:T(8,128)(2,1)S(1)}, bf16[512,512]{1,0:T(8,128)(2,1)S(1)}, u32[]{:S(2)}, u32[]{:S(2)}) collective-permute-start(bf16[512,512]{1,0:T(8,128)(2,1)S(1)} %shard_map.108.refs_0_), channel_id=1, source_target_pairs={{128,0},{192,64},{0,128},{64,192},{129,1},{193,65},{1,129},{65,193... | collective-permute-start | bytes 1572872 | tf_op jit(solution)/shard_map/ppermute | solution.py:104
  157.9 24.7 %collective-permute-start.28 = (bf16[512,512]{1,0:T(8,128)(2,1)S(1)}, bf16[512,512]{1,0:T(8,128)(2,1)S(1)}, u32[]{:S(2)}, u32[]{:S(2)}) collective-permute-start(bf16[512,512]{1,0:T(8,128)(2,1)S(1)} %shard_map.108.refs_0_), channel_id=1, source_target_pairs={{192,0},{0,64},{64,128},{128,192},{193,1},{1,65},{65,129},{129,193... | collective-permute-start | bytes 1572872 | tf_op jit(solution)/shard_map/ppermute | solution.py:104
  186.9 49.8 %all-to-all-start = ((bf16[8,112,512]{2,1,0:T(8,128)(2,1)}), bf16[8,112,512]{2,1,0:T(8,128)(2,1)S(1)}, u32[]{:S(2)}, u32[]{:S(2)}) async-start(bf16[8,112,512]{2,1,0:T(8,128)(2,1)} %get-tuple-element.72), calls=%async_computation | async-start | bytes 1835008 | tf_op jit(solution)/shard_map/all_to_all | solution.py:497
  192.8 51.0 %collective-permute-start.30 = (bf16[256,1024]{1,0:T(8,128)(2,1)}, bf16[256,1024]{1,0:T(8,128)(2,1)}, u32[]{:S(2)}, u32[]{:S(2)}) collective-permute-start(bf16[256,1024]{1,0:T(8,128)(2,1)} %copy-done.19), channel_id=1, source_target_pairs={{8,0},{16,8},{24,16},{0,24},{9,1},{17,9},{25,17},{1,25},{10,2},{18... | collective-permute-start | bytes 1572872 | tf_op jit(solution)/shard_map/ppermute | solution.py:108
  195.5 48.3 %collective-permute-start.31 = (bf16[256,1024]{1,0:T(8,128)(2,1)}, bf16[256,1024]{1,0:T(8,128)(2,1)}, u32[]{:S(2)}, u32[]{:S(2)}) collective-permute-start(bf16[256,1024]{1,0:T(8,128)(2,1)} %copy-done.18), channel_id=1, source_target_pairs={{16,0},{24,8},{0,16},{8,24},{17,1},{25,9},{1,17},{9,25},{18,2},{26... | collective-permute-start | bytes 1572872 | tf_op jit(solution)/shard_map/ppermute | solution.py:108
  195.8 47.9 %collective-permute-start.32 = (bf16[256,1024]{1,0:T(8,128)(2,1)}, bf16[256,1024]{1,0:T(8,128)(2,1)}, u32[]{:S(2)}, u32[]{:S(2)}) collective-permute-start(bf16[256,1024]{1,0:T(8,128)(2,1)} %copy-done.17), channel_id=1, source_target_pairs={{24,0},{0,8},{8,16},{16,24},{25,1},{1,9},{9,17},{17,25},{26,2},{2,... | collective-permute-start | bytes 1572872 | tf_op jit(solution)/shard_map/ppermute | solution.py:108
  238.2 13.5 %collective-permute-start.29 = (f32[56,512]{1,0:T(8,128)S(1)}, f32[56,512]{1,0:T(8,128)S(1)}, u32[]{:S(2)}, u32[]{:S(2)}) collective-permute-start(f32[56,512]{1,0:T(8,128)S(1)} %get-tuple-element.74), channel_id=1, source_target_pairs={{0,32},{32,0},{1,33},{33,1},{2,34},{34,2},{3,35},{35,3},{4,36},{36... | collective-permute-start | bytes 344072 | tf_op jit(solution)/shard_map/ppermute | solution.py:100
  (29 other events, 324.9 us)
